TPU v7x, 32 devices: a whole 2x2x4 slice. The times are simulated.
32 devices in a mesh: grp: 8 (over y, x, core), hd: 4 (over z).
Axes of the slice: x: 2, y: 2, z: 4, core: 2. Of those that a mesh axis runs over, the one named last changes fastest.
Arguments:
- pixels: bfloat16 [96, 256, 1024], P(('grp', 'hd')), may hold values from -6 to 6
- latents: bfloat16 [96, 256, 1024], P(('grp', 'hd')), may hold values from -6 to 6
- skip: bfloat16 [96, 256, 1024], P(('grp', 'hd')), may hold values from -6 to 6
- counts: int32 [96], P('grp'), may hold values from 1 to 256, as said below
- cotangent: bfloat16 [96, 256, 1024], P(('grp', 'hd')), may hold values from -6 to 6
- attn_in: float32 [6, 1024, 1024], P(None, None, ('grp', 'hd')), may hold values from -0.1875 to 0.1875
- attn_out: float32 [2, 1024, 1024], P(None, None, ('grp', 'hd')), may hold values from -2 to 2
- w_in: float32 [1024, 4096], P(None, ('grp', 'hd')), may hold values from -0.1875 to 0.1875
- w_out: float32 [4096, 1024], P(None, ('grp', 'hd')), may hold values from -0.09375 to 0.09375
- gains: float32 [4, 1024], P(None, ('grp', 'hd')), may hold values from 0.5 to 1.5
- attn_in_first: float32 [6, 1024, 1024], P(None, None, ('grp', 'hd')), may hold values from -896 to 896
- attn_in_second: float32 [6, 1024, 1024], P(None, None, ('grp', 'hd')), may hold values from 12288 to 196608
- attn_out_first: float32 [2, 1024, 1024], P(None, None, ('grp', 'hd')), may hold values from -80 to 80
- attn_out_second: float32 [2, 1024, 1024], P(None, None, ('grp', 'hd')), may hold values from 96 to 1536
- w_in_first: float32 [1024, 4096], P(None, ('grp', 'hd')), may hold values from -256 to 256
- w_in_second: float32 [1024, 4096], P(None, ('grp', 'hd')), may hold values from 1117 to 17873
- w_out_first: float32 [4096, 1024], P(None, ('grp', 'hd')), may hold values from -512 to 512
- w_out_second: float32 [4096, 1024], P(None, ('grp', 'hd')), may hold values from 4423 to 70778
- gains_first: float32 [4, 1024], P(None, ('grp', 'hd')), may hold values from -7524.8325 to 7524.8325
- gains_second: float32 [4, 1024], P(None, ('grp', 'hd')), may hold values from 12288 to 14155776, as said below
Outputs:
- latents_out: bfloat16 [96, 256, 1024], P(('grp', 'hd'))
- pixels_grad: float32 [96, 256, 1024], P(('grp', 'hd'))
- latents_grad: float32 [96, 256, 1024], P(('grp', 'hd'))
- attn_in_moment: float32 [6, 1024, 1024], P(None, None, ('grp', 'hd'))
- attn_in_square: float32 [6, 1024, 1024], P(None, None, ('grp', 'hd'))
- attn_in_new: float32 [6, 1024, 1024], P(None, None, ('grp', 'hd'))
- attn_out_moment: float32 [2, 1024, 1024], P(None, None, ('grp', 'hd'))
- attn_out_square: float32 [2, 1024, 1024], P(None, None, ('grp', 'hd'))
- attn_out_new: float32 [2, 1024, 1024], P(None, None, ('grp', 'hd'))
- w_in_moment: float32 [1024, 4096], P(None, ('grp', 'hd'))
- w_in_square: float32 [1024, 4096], P(None, ('grp', 'hd'))
- w_in_new: float32 [1024, 4096], P(None, ('grp', 'hd'))
- w_out_moment: float32 [4096, 1024], P(None, ('grp', 'hd'))
- w_out_square: float32 [4096, 1024], P(None, ('grp', 'hd'))
- w_out_new: float32 [4096, 1024], P(None, ('grp', 'hd'))
- gains_moment: float32 [4, 1024], P(None, ('grp', 'hd'))
- gains_square: float32 [3, 1024], P(None, ('grp', 'hd'))
- mlp_gain_square: float32 [1024], P(('grp', 'hd'))
- gains_new: float32 [4, 1024], P(None, ('grp', 'hd'))
Inputs may be any that keep to these rules, and one draw needn't show every extreme that they name: The first counts[i] input rows of image i are visible, the rest are padding; some image has all 256 rows visible. `gains_second`: entries are positive.
All inputs are finite; a program needn't handle non-finite values.
Results may differ from a plain program's by a relative error of at most 0.029.
Values may be sent and summed in bfloat16 or wider, within the bound.
No kernel may reach another device: no remote copies, remote signals or barrier semaphores. Data moves between devices by JAX's collectives and lax.ppermute only.
A program may use at most 320 MiB of HBM per device.

v0:
```python
import functools

import jax
import jax.numpy as jnp
from jax import lax
from jax.experimental import pallas as pl
from jax.experimental.pallas import tpu as pltpu
from jax.sharding import PartitionSpec as P

NH = 8
STEP = 5
AXES = ("grp", "hd")

MIB = 1 << 20
F32, LOW = jnp.float32, jnp.bfloat16
VMEM = pl.BlockSpec(memory_space=pltpu.VMEM)
SMEM = pl.BlockSpec(memory_space=pltpu.SMEM)


ANY = pl.BlockSpec(memory_space=pl.ANY)


def adamw(weight, grad, first_old, second_old, learn_rate, decay):
    first_new = 0.5 * first_old + 0.5 * grad
    second_new = 0.5 * second_old + 0.5 * grad * grad
    correction = 1.0 - 0.5**STEP
    normed_step = first_new / correction / (jnp.sqrt(second_new / correction) + 1e-08)
    return (first_new, second_new, weight - learn_rate * (normed_step + decay * weight))


def log2(n):
    return n.bit_length() - 1


def outer_bits(groups, depth):
    first, last = log2(depth) + 1, log2(depth) + log2(groups)
    middle = (first + last) // 2
    return list(range(first, middle)), list(range(middle, last))


def swap(block, bit, total):
    return lax.ppermute(block, AXES, [(j, j ^ (1 << bit)) for j in range(total)])


def spread_of(order, core, total):
    bits = list(order) + [core]
    return tuple(sum(((p >> t) & 1) << b for t, b in enumerate(bits)) for p in range(total))


def added(a, b):
    return (a.astype(F32) + b.astype(F32)).astype(LOW)


def device_index():
    return lax.axis_index("grp") * lax.axis_size("hd") + lax.axis_index("hd")


def gather_steps(shard, order, core, total):
    held = shard
    for bit in order[:-1]:
        (came,) = yield [functools.partial(swap, held, bit, total)]
        held = jnp.concatenate([held, came], axis=0)
    (came,) = yield [functools.partial(swap, held, order[-1], total)]
    first, second = yield [functools.partial(swap, held, core, total), functools.partial(swap, came, core, total)]
    return [held, came, first, second]


def gather_gains_steps(gains, x_bit, y_bit, core, total):
    rows = gains.shape[0]
    held = gains.astype(LOW).reshape(1, -1)
    outer = (x_bit, y_bit)
    masks = [1 << x_bit, 1 << y_bit, (1 << x_bit) | (1 << y_bit)]
    exchange = lambda mask: functools.partial(lax.ppermute, held, AXES, [(j, j ^ mask) for j in range(total)])
    came = yield [exchange(mask) for mask in masks]
    held = jnp.concatenate([held, *came], axis=0)
    for bit in (1, 0, core):
        (came,) = yield [functools.partial(swap, held, bit, total)]
        held = jnp.concatenate([held, came], axis=0)
    owners = jnp.array(spread_of((*outer, 1, 0), core, total), jnp.int32) ^ device_index()
    place = lax.broadcasted_iota(jnp.int32, (total, total), 0) == owners[None, :]
    every = jnp.dot(place.astype(LOW), held, preferred_element_type=F32)
    return jnp.swapaxes(every.reshape(total, rows, -1), 0, 1).reshape(rows, -1)


def scatter_steps(mine, theirs, x_bit, y_bit, core, total, last=False):
    (came,) = yield [functools.partial(swap, theirs, core, total)]
    half = mine.shape[1] // 2
    away = [added(mine[k, half:], came[k, half:]) for k in range(2)]
    held = [added(mine[k, :half], came[k, :half]) for k in range(2)]
    came = yield [functools.partial(swap, block, bit, total) for block, bit in zip(away, (y_bit, x_bit))]
    half //= 2
    away = [added(held[k][half:], came[k][half:]) for k in range(2)]
    held = [added(held[k][:half], came[k][:half]) for k in range(2)]
    came = yield [functools.partial(swap, block, bit, total) for block, bit in zip(away, (x_bit, y_bit))]
    both = jnp.stack([added(held[k], came[k]) for k in range(2)], axis=1)
    if last:
        (came,) = yield [functools.partial(lax.all_to_all, both, "hd", 0, 0, tiled=True)]
        return jnp.sum(came.astype(F32), axis=0)
    for bit in range(core):
        half = both.shape[0] // 2
        (came,) = yield [functools.partial(swap, both[half:], bit, total)]
        both = added(both[:half], came)
    return both[0].astype(F32)


class Chain:
    def __init__(self, steps):
        self.steps, self.result, self.under_way = steps, None, None
        self.wanted = next(steps)

    def start(self):
        if self.under_way is None:
            self.under_way = [exchange() for exchange in self.wanted]

    def advance(self, came):
        self.under_way = None
        try:
            self.wanted = self.steps.send(came)
        except StopIteration as stop:
            self.wanted, self.result = [], stop.value


def in_round(chains, compute=None, *, beside=None, longer=()):
    chains = [chain for chain in chains if chain.wanted]
    for chain in chains:
        chain.start()
    ending = [chain for chain in chains if chain not in longer]
    done = compute() if compute else ()
    came, done, beside = lax.optimization_barrier(([chain.under_way for chain in ending], done, beside))
    for chain, blocks in zip(ending, came):
        chain.advance(blocks)
    return done if beside is None else (done, beside)


def place_blocks(refs, spread, dst, rows, sem):
    if spread is None:
        pltpu.make_async_copy(refs[0].at[:, rows], dst, sem).start()
        return
    me, each = device_index(), len(spread) // 4
    for p, mask in enumerate(spread):
        pltpu.make_async_copy(refs[p // each].at[p % each, rows], dst.at[me ^ mask], sem).start()


def z_place(mask, owner, depth, last):
    if last:
        return owner & (depth - 1)
    return sum(((mask >> bit) & 1) << (log2(depth) - 1 - bit) for bit in range(log2(depth)))


def cut_blocks(halves, refs, depth, sems, last=False):
    me = device_index()
    for mask in range(32):
        owner = me ^ mask
        place = mask // (2 * depth)
        for half, src_of, rows in halves:
            group = place if half == 0 else place // 2 + place % 2 * 2
            dst = refs[mask // depth % 2].at[half, group * depth + z_place(mask, owner, depth, last)]
            dst = dst if rows is None else dst.at[rows]
            pltpu.make_async_copy(src_of(owner), dst, sems.at[mask // depth % 2]).start()


def bring(src, dst, sem):
    copy = pltpu.make_async_copy(src, dst, sem)
    copy.start()
    return copy


def await_whole(refs, sems):
    for at, ref in enumerate(refs):
        pltpu.make_async_copy(ref, ref, sems.at[at]).wait()


def blocks_of(shape):
    return [jax.ShapeDtypeStruct((2, 16, *shape), LOW)] * 2


BLOCK = 512
PARTS = 4
CALLS = 2


def pack_kernel(attn_in_ref, attn_out_ref, w_out_ref, w_in_ref, *refs):
    cross, own, cross_out, own_out, mlp, attn_in, attn_out, w_out, w_in, sems = refs
    sources, places = (attn_in_ref, attn_out_ref, w_in_ref, w_out_ref), (attn_in, attn_out, w_in, w_out)
    for copy in [bring(src, dst, sems.at[at]) for at, (src, dst) in enumerate(zip(sources, places))]:
        copy.wait()
    rows = attn_in.shape[1]
    for at, (to, to_out) in enumerate(((cross, cross_out), (own, own_out))):
        for m in range(3):
            to[0, m * rows : (m + 1) * rows, :] = attn_in[3 * at + m].astype(LOW)
        to_out[0] = attn_out[at].astype(LOW)
    width = w_out.shape[1] // PARTS
    for c in range(PARTS):
        mlp[c * rows : (c + 1) * rows, :] = w_out[:, c * width : (c + 1) * width].astype(LOW)
    mlp[PARTS * rows :, :] = w_in[...].T.astype(LOW)


def pack(attn_in_t, attn_out_t, w_out_t, w_in):
    rows, width = attn_in_t.shape[1:]
    return pl.pallas_call(
        pack_kernel,
        out_shape=[jax.ShapeDtypeStruct((1, 3 * rows, width), LOW)] * 2
        + [jax.ShapeDtypeStruct((1, rows, width), LOW)] * 2
        + [jax.ShapeDtypeStruct((PARTS * rows + w_in.shape[1], width), LOW)],
        in_specs=[ANY] * 4,
        out_specs=[VMEM] * 5,
        scratch_shapes=[pltpu.VMEM(a.shape, F32) for a in (attn_in_t, attn_out_t, w_out_t, w_in)]
        + [pltpu.SemaphoreType.DMA((4,))],
        compiler_params=pltpu.CompilerParams(vmem_limit_bytes=16 * MIB),
    )(attn_in_t, attn_out_t, w_out_t, w_in)


def from_all(own):
    total = lax.axis_size("grp") * lax.axis_size("hd")
    return lax.all_to_all(jnp.broadcast_to(own[None], (total, *own.shape)), AXES, 0, 0, tiled=True)


def gather_gains(gains):
    rows = gains.shape[0]
    every = from_all(gains.astype(LOW).reshape(-1)).astype(F32)
    return jnp.swapaxes(every.reshape(every.shape[0], rows, -1), 0, 1).reshape(rows, -1)


def scatter_gains(grads):
    total = lax.axis_size("grp") * lax.axis_size("hd")
    rows = grads.shape[0]
    blocks = jnp.swapaxes(grads.reshape(rows, total, -1), 0, 1).reshape(total, -1)
    came = lax.all_to_all(blocks, AXES, 0, 0, tiled=True)
    return jnp.sum(came, axis=0).reshape(rows, -1)


def dot_nn(a, b):
    return lax.dot_general(a, b, (((1,), (0,)), ((), ())), preferred_element_type=F32)


def dot_nt(a, b):
    return lax.dot_general(a, b, (((1,), (1,)), ((), ())), preferred_element_type=F32)


def dot_tn(a, b):
    return lax.dot_general(a, b, (((0,), (0,)), ((), ())), preferred_element_type=F32)


ROWS = 32


def unit_rows(rows):
    inverse = lax.rsqrt(jnp.mean(rows * rows, axis=-1, keepdims=True) + 1e-06)
    return rows * inverse, inverse


def normalise(source, gain, out):
    for at in range(0, source.shape[0], ROWS):
        span = slice(at, at + ROWS)
        out[span, :] = (unit_rows(source[span, :].astype(F32))[0] * gain).astype(LOW)


def norm_grad(source, gain, upstream, base, out, first=0):
    gain_grad = 0.0
    for at in range(0, upstream.shape[0], ROWS):
        span = slice(first + at, first + at + ROWS)
        unit, inverse = unit_rows(source[span, :].astype(F32))
        grad = upstream[at : at + ROWS]
        scaled = grad * gain
        inner = jnp.mean(scaled * unit, axis=-1, keepdims=True)
        extra = (scaled - unit * inner) * inverse
        out[span, :] = extra if base is None else base[span, :].astype(F32) + extra
        gain_grad += jnp.sum((grad * unit).reshape(ROWS // 8, 8, -1), axis=0)
    return jnp.sum(gain_grad, axis=0, keepdims=True)


SHARES = 2


def in_shares(rows, work, scratch, out, sem):
    count = rows // SHARES
    for at in range(0, rows, count):
        work(at, count)
        bring(scratch.at[at : at + count], out.at[at : at + count], sem)


def head_scores(query, key, count, scale):
    scores = dot_nt(query, key) * scale
    if count is not None:
        place = lax.broadcasted_iota(jnp.int32, scores.shape, 1)
        scores = jnp.where(place < count, scores, -1e30)
    return scores


def matrix(weights):
    return weights[...].reshape(-1, weights.shape[2])


def attend_kernel(cross, images, size, spreads, *refs):
    if cross:
        counts, gains, source, target, *refs = refs
    else:
        gains, target, *refs = refs
    *pieces, q_out, k_out, v_out, context_out, sum_out, log_out, whole, refs = *refs[:-14], *refs[-14:-7], refs[-7:]
    kept, target_v, source_v, weights, normal, total, sems = refs
    q_v, k_v, v_v, context_v = (kept.at[m] for m in range(4))
    rows = weights.shape[2]
    count = len(pieces) // 2
    come = [bring(source, source_v, sems.at[4])] if cross else []
    come.append(bring(target, target_v, sems.at[5]))
    for m in (1, 2, 0):
        place_blocks(pieces[:count], spreads[0], weights.at[m], pl.ds(m * rows, rows), sems.at[m])
    place_blocks(pieces[count:], spreads[1], weights.at[3], slice(None), sems.at[3])

    def arrived(m):
        pltpu.make_async_copy(weights.at[m], weights.at[m], sems.at[m]).wait()
        return matrix(weights.at[m])

    key_gain, query_gain = (0, 1) if cross else (2, 2)
    come[0].wait()
    normalise(source_v if cross else target_v, gains[key_gain : key_gain + 1, :], normal)
    k_v[...] = dot_nt(normal[...], arrived(1)).astype(LOW)
    leave = [bring(k_v, k_out, sems.at[6])]
    v_v[...] = dot_nt(normal[...], arrived(2)).astype(LOW)
    leave.append(bring(v_v, v_out, sems.at[7]))
    if cross:
        come[1].wait()
        normalise(target_v, gains[query_gain : query_gain + 1, :], normal)
    q_v[...] = dot_nt(normal[...], arrived(0)).astype(LOW)
    leave.append(bring(q_v, q_out, sems.at[8]))
    out_weights = arrived(3)
    leave.append(bring(weights, whole, sems.at[9]))
    width = q_v.shape[1] // NH
    scale = width ** (-0.5)

    def one_image(image, carry):
        span = pl.ds(pl.multiple_of(image * size, size), size)
        count = counts[image] if cross else None
        for h in range(NH):
            part = slice(h * width, (h + 1) * width)
            scores = head_scores(q_v[span, part], k_v[span, part], count, scale)
            highest = jnp.max(scores, axis=-1, keepdims=True)
            exponent = jnp.exp(scores - highest)
            row_total = jnp.sum(exponent, axis=-1, keepdims=True)
            probs = (exponent * (1.0 / row_total)).astype(LOW)
            context_v[span, part] = dot_nn(probs, v_v[span, part]).astype(LOW)
            log_out[span, h : h + 1] = highest + jnp.log(row_total)
        return carry

    lax.fori_loop(0, images, one_image, 0)
    leave.append(bring(context_v, context_out, sems.at[10]))

    def work(at, count):
        span = slice(at, at + count)
        total[span, :] = target_v[span, :].astype(F32) + dot_nt(context_v[span, :], out_weights)

    in_shares(total.shape[0], work, total, sum_out, sems.at[11])
    for copy in leave:
        copy.wait()
    pltpu.make_async_copy(total, sum_out, sems.at[11]).wait()


def attend_block(gains, source, target, counts, pieces, spreads, images):
    cross = source is not None
    rows, width = target.shape
    low = jax.ShapeDtypeStruct((rows, width), LOW)
    weights = (4, 32, width // 32, width)
    head = (counts, gains, source, target) if cross else (gains, target)
    return pl.pallas_call(
        functools.partial(attend_kernel, cross, images, rows // images, spreads),
        out_shape=[low] * 4
        + [jax.ShapeDtypeStruct(shape, F32) for shape in ((rows, width), (rows, NH))]
        + [jax.ShapeDtypeStruct(weights, LOW)],
        in_specs=([SMEM] if cross else []) + [VMEM] + [ANY] * (2 if cross else 1) + [ANY] * len(pieces),
        out_specs=[ANY] * 5 + [VMEM, ANY],
        scratch_shapes=[
            pltpu.VMEM((4, rows, width), LOW),
            pltpu.VMEM((rows, width), target.dtype),
            pltpu.VMEM((rows if cross else 8, width), LOW),
            pltpu.VMEM(weights, LOW),
            pltpu.VMEM((rows, width), LOW),
            pltpu.VMEM((rows, width), F32),
            pltpu.SemaphoreType.DMA((12,)),
        ],
        compiler_params=pltpu.CompilerParams(vmem_limit_bytes=48 * MIB),
        cost_estimate=pl.CostEstimate(
            flops=8 * rows * width * width + 4 * rows * width * (rows // images),
            bytes_accessed=12 * rows * width + 8 * width * width,
            transcendentals=rows * NH * (rows // images),
        ),
    )(*head, *pieces)


def scores_grad_kernel(cross, images, size, *refs):
    if cross:
        counts, *refs = refs
    upstream, q_in, k_in, v_in, context_in, log_in, whole, *refs = refs
    grads_out, (up_v, kept, grads, dc, wo_v, sems) = refs[:3], refs[3:]
    come = [bring(upstream, up_v, sems.at[0]), bring(whole.at[3], wo_v, sems.at[1])]
    come += [bring(src, kept.at[m], sems.at[2 + m]) for m, src in enumerate((q_in, k_in, v_in, context_in))]
    q_v, k_v, v_v, context_v = (kept.at[m] for m in range(4))
    dq, dk, dv = (grads.at[m] for m in range(3))
    for copy in come[:2]:
        copy.wait()
    dc[...] = dot_nn(up_v[...].astype(LOW), matrix(wo_v)).astype(LOW)
    for copy in come[2:]:
        copy.wait()
    width = q_v.shape[1] // NH
    scale = width ** (-0.5)

    def one_image(image, carry):
        span = pl.ds(pl.multiple_of(image * size, size), size)
        count = counts[image] if cross else None
        for h in range(NH):
            part = slice(h * width, (h + 1) * width)
            query, key, value, grad = q_v[span, part], k_v[span, part], v_v[span, part], dc[span, part]
            probs = jnp.exp(head_scores(query, key, count, scale) - log_in[span, h : h + 1])
            prob_grad = dot_nt(grad, value)
            dv[span, part] = dot_tn(probs.astype(LOW), grad).astype(LOW)
            inner = jnp.sum(grad.astype(F32) * context_v[span, part].astype(F32), axis=-1, keepdims=True)
            score_grad = (probs * (prob_grad - inner)).astype(LOW)
            dq[span, part] = (dot_nn(score_grad, key) * scale).astype(LOW)
            dk[span, part] = (dot_tn(score_grad, query) * scale).astype(LOW)
        for m, to in enumerate(grads_out):
            pltpu.make_async_copy(grads.at[m, span], to.at[span], sems.at[6 + m]).start()
        return carry

    lax.fori_loop(0, images, one_image, 0)
    await_whole(grads_out, sems.at[pl.ds(6, 3)])


def scores_grad(counts, upstream, saved, whole, images):
    cross = counts is not None
    rows, width = upstream.shape
    return pl.pallas_call(
        functools.partial(scores_grad_kernel, cross, images, rows // images),
        out_shape=[jax.ShapeDtypeStruct((rows, width), LOW)] * 3,
        in_specs=([SMEM] if cross else []) + [ANY] * 5 + [VMEM, ANY],
        out_specs=[ANY] * 3,
        scratch_shapes=[
            pltpu.VMEM((rows, width), F32),
            pltpu.VMEM((4, rows, width), LOW),
            pltpu.VMEM((3, rows, width), LOW),
            pltpu.VMEM((rows, width), LOW),
            pltpu.VMEM(whole.shape[1:], LOW),
            pltpu.SemaphoreType.DMA((9,)),
        ],
        compiler_params=pltpu.CompilerParams(vmem_limit_bytes=48 * MIB),
        cost_estimate=pl.CostEstimate(
            flops=2 * rows * width * width + 10 * rows * width * (rows // images),
            bytes_accessed=18 * rows * width + 4 * width * width,
            transcendentals=rows * NH * (rows // images),
        ),
    )(*([counts] if cross else []), upstream, *saved, whole)


def matrix_shares(count, rows):
    shares = []
    for m in range(count // 2 * 2):
        shares.append((m % 2, m, 0, rows, m // 2 * rows))
    if count % 2:
        for half in range(2):
            shares.append((half, count - 1, half * rows // 2, rows // 2, count // 2 * rows))
    return shares


def matrix_blocks(sums, count, rows):
    parts = [[] for _ in range(count)]
    for half, m, _, length, at in matrix_shares(count, rows):
        parts[m].append(sums[half, at : at + length])
    return [part[0] if len(part) == 1 else jnp.concatenate(part, axis=0) for part in parts]


def matrix_grad_kernel(cross, depth, *refs):
    gains, *refs = refs
    ins, (*outs, target_v, source_v, up_v, kept, grads, normal, sems, send_sems) = refs[: 6 + cross], refs[6 + cross :]
    to = [source_v] * cross + [target_v, up_v] + [kept.at[m] for m in (3, 0, 1, 2)]
    order = (1, 4, 0, 5, 6, 2, 3) if cross else (0, 3, 4, 5, 1, 2)
    come = {at: bring(ins[at], to[at], sems.at[at]) for at in order}
    dq, dk, dv, context = (kept.at[m] for m in range(4))
    key_gain, query_gain = (0, 1) if cross else (2, 2)
    width = target_v.shape[1]

    def finish(m, grad):
        grads[m] = grad.astype(LOW)
        if depth is None:
            bring(grads.at[m], outs[m], send_sems.at[m])
            return
        rows = width // 32

        def part(first, count):
            return lambda owner: grads.at[m, pl.ds(pl.multiple_of(owner * rows + first, count), count), :]

        halves = [
            (half, part(first, count), pl.ds(at, count))
            for half, m_at, first, count, at in matrix_shares(grads.shape[0], rows)
            if m_at == m
        ]
        cut_blocks(halves, outs, depth, send_sems, last=cross)

    come[cross].wait()
    normalise(target_v, gains[query_gain : query_gain + 1, :], normal)
    come[3 + cross].wait()
    finish(0, dot_tn(dq[...], normal[...]))
    if cross:
        come[0].wait()
        normalise(source_v, gains[key_gain : key_gain + 1, :], normal)
    come[4 + cross].wait()
    finish(1, dot_tn(dk[...], normal[...]))
    come[5 + cross].wait()
    finish(2, dot_tn(dv[...], normal[...]))
    come[1 + cross].wait()
    come[2 + cross].wait()
    finish(3, dot_tn(up_v[...].astype(LOW), context[...]))
    await_whole(outs, send_sems)


def matrix_grads(gains, source, target, upstream, context, score_grads, depth):
    cross = source is not None
    rows, width = target.shape
    head = (gains, source, target) if cross else (gains, target)
    count = 4
    if depth is None:
        out_shape = [jax.ShapeDtypeStruct((width, width), LOW)] * count
    else:
        out_shape = blocks_of((count * width // 64, width))
    return pl.pallas_call(
        functools.partial(matrix_grad_kernel, cross, depth),
        out_shape=out_shape,
        in_specs=[VMEM] + [ANY] * (len(head) + 4),
        out_specs=[ANY] * len(out_shape),
        scratch_shapes=[
            pltpu.VMEM((rows, width), target.dtype),
            pltpu.VMEM((rows if cross else 8, width), LOW),
            pltpu.VMEM((rows, width), F32),
            pltpu.VMEM((4, rows, width), LOW),
            pltpu.VMEM((count, width, width), LOW),
            pltpu.VMEM((rows, width), LOW),
            pltpu.SemaphoreType.DMA((7,)),
            pltpu.SemaphoreType.DMA((len(out_shape),)),
        ],
        compiler_params=pltpu.CompilerParams(vmem_limit_bytes=48 * MIB),
        cost_estimate=pl.CostEstimate(
            flops=2 * count * rows * width * width,
            bytes_accessed=16 * rows * width + 2 * count * width * width,
            transcendentals=rows,
        ),
    )(*head, upstream, context, *score_grads)


def project_grad_kernel(cross, *refs):
    gains, *refs = refs
    ins, refs = refs[: 6 + cross], refs[6 + cross :]
    outs = 1 + cross
    grads_out, gain_outs, (target_v, source_v, up_v, kept, weights, result, sems) = refs[:outs], refs[outs : 2 * outs], refs[2 * outs :]
    whole = ins[-1]
    inputs = list(ins[:-1])
    to = [source_v] * cross + [target_v, up_v] + [kept.at[m] for m in range(3)]
    order = (3, 1, 2, 4, 5, 0) if cross else (2, 3, 4, 0, 1)
    come, used = {}, 0
    for at in order:
        come[at] = bring(inputs[at], to[at], sems.at[at])
        if at >= 2 + cross:
            m = at - 2 - cross
            come["w%d" % m] = bring(whole.at[m], weights.at[m], sems.at[6 + m])
    dq, dk, dv = (kept.at[m] for m in range(3))
    key_gain, query_gain = (0, 1) if cross else (2, 2)
    rows = target_v.shape[0]

    def back_through(members, few):
        return sum(dot_nn(kept[m, few, :], matrix(weights.at[m])) for m in members)

    def shares(which, members, source, gain, base):
        gain_grads = []

        def work(at, count):
            back = back_through(members, slice(at, at + count))
            gain_grads.append(norm_grad(source, gain, back, base, result.at[which], at))

        in_shares(rows, work, result.at[which], grads_out[which], sems.at[9 + which])
        gain_outs[which][...] = sum(gain_grads)

    def arrived(*names):
        for name in names:
            come[name].wait()

    if cross:
        arrived(3, "w0", 1, 2)
        shares(0, (0,), target_v, gains[query_gain : query_gain + 1, :], up_v)
        arrived(4, "w1", 5, "w2", 0)
        shares(1, (1, 2), source_v, gains[key_gain : key_gain + 1, :], None)
    else:
        arrived(2, "w0", 3, "w1", 4, "w2", 0, 1)
        shares(0, (0, 1, 2), target_v, gains[key_gain : key_gain + 1, :], up_v)
    for which in range(outs):
        pltpu.make_async_copy(result.at[which], grads_out[which], sems.at[9 + which]).wait()


def project_grad(gains, source, target, upstream, score_grads, whole):
    cross = source is not None
    rows, width = target.shape
    outs = 2 if cross else 1
    head = (gains, source, target) if cross else (gains, target)
    result = pl.pallas_call(
        functools.partial(project_grad_kernel, cross),
        out_shape=[jax.ShapeDtypeStruct((rows, width), F32)] * outs + [jax.ShapeDtypeStruct((1, width), F32)] * outs,
        in_specs=[VMEM] + [ANY] * (len(head) + 4),
        out_specs=[ANY] * outs + [VMEM] * outs,
        scratch_shapes=[
            pltpu.VMEM((rows, width), target.dtype),
            pltpu.VMEM((rows if cross else 8, width), LOW),
            pltpu.VMEM((rows, width), F32),
            pltpu.VMEM((3, rows, width), LOW),
            pltpu.VMEM((3, *whole.shape[1:]), LOW),
            pltpu.VMEM((outs, rows, width), F32),
            pltpu.SemaphoreType.DMA((11,)),
        ],
        compiler_params=pltpu.CompilerParams(vmem_limit_bytes=48 * MIB),
        cost_estimate=pl.CostEstimate(
            flops=6 * rows * width * width, bytes_accessed=20 * rows * width + 6 * width * width, transcendentals=rows
        ),
    )(*head, upstream, *score_grads, whole)
    return result[:outs], result[outs:]


def mlp_forward_kernel(call, depth, second, cotangent, *refs):
    if call == 0:
        gain_row, bands, normal_out, sum_out, hidden_out, *refs = refs
    else:
        normal_in, skip, bands, sum_out, hidden_out, *refs = refs
    *outs, second_v, cot_v, extra_v, normal, cot_t, active, hidden_grad, result, lower_v, lift_v, grad_v, sems, send_sems = refs
    parts, rows, size = lower_v.shape[0], lower_v.shape[2], lower_v.shape[3]
    count, units = lift_v.shape[:2]
    steps = range(0, parts * size, BLOCK)
    share = BLOCK // units

    def bring_lift(step):
        here = pl.ds(step * share, share)
        there = bands.at[pl.ds(call * count + step * share, share), pl.ds(PARTS * rows, units)]
        return bring(there, lift_v.at[here], sems.at[4 + step])

    def bring_lower(c):
        return bring(bands.at[:, pl.ds((call * parts + c) * rows, rows)], lower_v.at[c], sems.at[8 + c])

    if call == 0:
        come = [bring(second, second_v, sems.at[0])]
    else:
        come = [bring(normal_in, normal, sems.at[0])]
    lifts = [bring_lift(0)]
    come.append(bring(cotangent, cot_v, sems.at[1]))
    lowers = [bring_lower(0)]
    lifts += [bring_lift(step) for step in range(1, len(steps))]
    lowers += [bring_lower(c) for c in range(1, parts)]
    if call == 1:
        come += [bring(second, second_v, sems.at[2]), bring(skip, extra_v, sems.at[3])]
    leave = []
    come[0].wait()
    if call == 0:
        normalise(second_v, gain_row[...], normal)
        leave.append(bring(normal, normal_out, sems.at[2]))
    for step, start in enumerate(steps):
        lifts[step].wait()
        hidden = dot_nt(normal[...], lift_v[step * share : (step + 1) * share].reshape(BLOCK, -1))
        if step == 0:
            come[1].wait()
        if start % size == 0:
            lowers[start // size].wait()
        columns = slice(start % size, start % size + BLOCK)
        upstream = dot_nn(cot_v[...], lower_v[start // size, :, :, columns].reshape(-1, BLOCK))
        for at in range(0, hidden.shape[0], ROWS):
            few = slice(at, at + ROWS)
            value = hidden[few]
            square = value * value
            root = 0.7978845608028654
            tanh = jnp.tanh(value * (root + (root * 0.044715) * square))
            half = 0.5 + 0.5 * tanh
            rise = (0.5 * value) * (1.0 - tanh * tanh) * (root + (3 * root * 0.044715) * square)
            active[few, start : start + BLOCK] = (value * half).astype(LOW)
            hidden_grad[few, start : start + BLOCK] = (upstream[few] * (half + rise)).astype(LOW)
        here = slice(start, start + BLOCK)
        bring(hidden_grad.at[:, here], hidden_out.at[:, here], sems.at[10])
        if step == 0:
            cot_t[...] = cot_v[...].T
        if (start + BLOCK) % size == 0:
            c = start // size
            columns = slice(c * size, (c + 1) * size)
            grad_v[:, columns] = dot_nn(cot_t[...], active[:, columns]).astype(LOW)
            if depth is None:
                bring(grad_v.at[:, columns], outs[0].at[:, columns], send_sems.at[0])
            else:
                src_of = lambda owner: grad_v.at[pl.ds(pl.multiple_of(owner * rows, rows), rows), columns]
                cut_blocks([(c, src_of, None)], outs, depth, send_sems)
    for copy in come[2:]:
        copy.wait()

    def work(at, length):
        few = slice(at, at + length)
        total = second_v[few, :]
        for c in range(parts):
            total = total + dot_nt(active[few, c * size : (c + 1) * size], matrix(lower_v.at[c]))
        result[few, :] = total if call == 0 else (total + extra_v[few, :].astype(F32)).astype(LOW)

    in_shares(result.shape[0], work, result, sum_out, sems.at[11])
    for copy in leave:
        copy.wait()
    pltpu.make_async_copy(result, sum_out, sems.at[11]).wait()
    pltpu.make_async_copy(hidden_grad, hidden_out, sems.at[10]).wait()
    await_whole(outs, send_sems)


def mlp_forward(call, second, cotangent, others, bands, hidden, depth):
    rows, width = second.shape
    units, parts = hidden // CALLS, PARTS // CALLS
    low = jax.ShapeDtypeStruct((rows, width), LOW)
    if depth is None:
        outs = [jax.ShapeDtypeStruct((width, units), LOW)]
    else:
        outs = blocks_of((width // 32, units // 2))
    return pl.pallas_call(
        functools.partial(mlp_forward_kernel, call, depth),
        out_shape=[low]
        + [jax.ShapeDtypeStruct((rows, width), F32)] * (call == 0)
        + [jax.ShapeDtypeStruct((rows, units), LOW)]
        + outs,
        in_specs=[ANY] * 2 + ([VMEM] if call == 0 else [ANY] * 2) + [ANY],
        out_specs=[ANY] * (3 if call == 0 else 2) + [ANY] * len(outs),
        scratch_shapes=[
            pltpu.VMEM((rows, width), F32),
            pltpu.VMEM((rows, width), LOW),
            pltpu.VMEM((8 if call == 0 else rows, width), LOW),
            pltpu.VMEM((rows, width), LOW),
            pltpu.VMEM((width, rows), LOW),
            pltpu.VMEM((rows, units), LOW),
            pltpu.VMEM((rows, units), LOW),
            pltpu.VMEM((rows, width), F32 if call == 0 else LOW),
            pltpu.VMEM((parts, 32, width // 32, units // parts), LOW),
            pltpu.VMEM((32 // CALLS, hidden // 32, width), LOW),
            pltpu.VMEM((width, units), LOW),
            pltpu.SemaphoreType.DMA((12,)),
            pltpu.SemaphoreType.DMA((len(outs),)),
        ],
        compiler_params=pltpu.CompilerParams(vmem_limit_bytes=56 * MIB),
        cost_estimate=pl.CostEstimate(
            flops=8 * rows * width * units,
            bytes_accessed=6 * width * units + 12 * rows * width + 2 * rows * units,
            transcendentals=rows * units,
        ),
    )(second, cotangent, *others, bands)


def mlp_backward_kernel(depth, gain_row, second, cotangent, normal, hidden_grad0, hidden_grad1, bands, *refs):
    second_grad, gain_grad, *refs = refs
    *outs, second_v, cot_v, normal_v, hidden_grads, normal_t, result, lift_v, grad_v, sems, send_sems = refs
    units = lift_v.shape[1]
    share, half = BLOCK // units, lift_v.shape[0] // 2
    come = [bring(normal, normal_v, sems.at[0])]
    come += [bring(src, hidden_grads.at[h], sems.at[1 + h]) for h, src in enumerate((hidden_grad0, hidden_grad1))]
    come.append(bring(bands.at[:, pl.ds(bands.shape[1] - units, units)], lift_v, sems.at[3]))
    come += [bring(second, second_v, sems.at[4]), bring(cotangent, cot_v, sems.at[5])]
    come[0].wait()
    normal_t[...] = normal_v[...].T
    steps = grad_v.shape[0] // 2
    for h in range(2):
        come[1 + h].wait()

        def one_block(at, carry):
            columns = pl.ds(pl.multiple_of(at * BLOCK, BLOCK), BLOCK)
            step = h * steps + at
            grad_v[step] = dot_nn(normal_t[...], hidden_grads[h, :, columns]).astype(LOW)
            if depth is None:
                columns = pl.ds(pl.multiple_of(step * BLOCK, BLOCK), BLOCK)
                pltpu.make_async_copy(grad_v.at[step], outs[0].at[:, columns], send_sems.at[0]).start()
                return carry
            size = grad_v.shape[1] // 2
            for c in range(share):
                mask = (step * share + c) ^ device_index()
                group = mask // (2 * depth)
                place = z_place(mask, None, depth, False)
                for away in range(2):

                    @pl.when((mask // depth) % 2 == away)
                    def send():
                        for part in range(2):
                            to = group if part == 0 else group // 2 + group % 2 * 2
                            pltpu.make_async_copy(
                                grad_v.at[step, part * size : (part + 1) * size, c * units : (c + 1) * units],
                                outs[away].at[part, to * depth + place],
                                send_sems.at[away],
                            ).start()

            return carry

        lax.fori_loop(0, steps, one_block, 0)
    for copy in come[3:]:
        copy.wait()
    gain_grads = []

    def work(at, count):
        few = slice(at, at + count)
        back = sum(
            dot_nn(hidden_grads[h, few, :], lift_v[h * half : (h + 1) * half].reshape(half * units, -1)) for h in range(2)
        )
        gain_grads.append(norm_grad(second_v, gain_row[...], back, cot_v, result, at))

    in_shares(result.shape[0], work, result, second_grad, sems.at[6])
    gain_grad[...] = sum(gain_grads)
    pltpu.make_async_copy(result, second_grad, sems.at[6]).wait()
    await_whole(outs, send_sems)


def mlp_backward(gain_row, second, cotangent, normal, hidden_grads, bands, hidden, depth):
    rows, width = second.shape
    if depth is None:
        outs = [jax.ShapeDtypeStruct((width, hidden), LOW)]
    else:
        outs = blocks_of((width // 2, hidden // 32))
    return pl.pallas_call(
        functools.partial(mlp_backward_kernel, depth),
        out_shape=[jax.ShapeDtypeStruct((rows, width), F32), jax.ShapeDtypeStruct((1, width), F32)] + outs,
        in_specs=[VMEM] + [ANY] * 6,
        out_specs=[ANY, VMEM] + [ANY] * len(outs),
        scratch_shapes=[
            pltpu.VMEM((rows, width), F32),
            pltpu.VMEM((rows, width), LOW),
            pltpu.VMEM((rows, width), LOW),
            pltpu.VMEM((2, rows, hidden // 2), LOW),
            pltpu.VMEM((width, rows), LOW),
            pltpu.VMEM((rows, width), F32),
            pltpu.VMEM((32, hidden // 32, width), LOW),
            pltpu.VMEM((hidden // BLOCK, width, BLOCK), LOW),
            pltpu.SemaphoreType.DMA((7,)),
            pltpu.SemaphoreType.DMA((len(outs),)),
        ],
        compiler_params=pltpu.CompilerParams(vmem_limit_bytes=56 * MIB),
        cost_estimate=pl.CostEstimate(
            flops=4 * rows * width * hidden,
            bytes_accessed=4 * width * hidden + 12 * rows * width + 2 * rows * hidden,
            transcendentals=0,
        ),
    )(gain_row, second, cotangent, normal, *hidden_grads, bands)


def local(
    pixels,
    latents,
    skip,
    counts,
    cotangent,
    attn_in,
    attn_out,
    w_in,
    w_out,
    gains,
    attn_in_first,
    attn_in_second,
    attn_out_first,
    attn_out_second,
    w_in_first,
    w_in_second,
    w_out_first,
    w_out_second,
    gains_first,
    gains_second,
):
    groups, depth = lax.axis_size("grp"), lax.axis_size("hd")
    total, core = groups * depth, log2(depth)
    fast = total == 32 and depth == 4
    images, size, width = latents.shape
    hidden = w_out.shape[0]
    flat = lambda rows: rows.reshape(-1, width)
    whole = lambda rows: rows.reshape(images, -1, width)
    pixel_rows, latent_rows, cot_rows = flat(pixels), flat(latents), flat(cotangent)
    attn_in_t, attn_out_t, w_out_t = jnp.swapaxes(attn_in, 1, 2), jnp.swapaxes(attn_out, 1, 2), w_out.T
    own_counts = lax.dynamic_slice_in_dim(counts, lax.axis_index("hd") * images, images)
    cut = depth if fast else None

    def cross_forward(pieces, spreads):
        return attend_block(gain_rows, pixel_rows, latent_rows, own_counts, pieces, spreads, images)

    def self_forward(pieces, spreads):
        return attend_block(gain_rows, None, first_sum, None, pieces, spreads, images)

    if fast:
        (x_bit,), (y_bit,) = outer_bits(groups, depth)
        *shards, mlp_shard = pack(attn_in_t, attn_out_t, w_out_t, w_in)
        orders = ((1, 0, x_bit, y_bit), (1, 0, y_bit, x_bit), (x_bit, y_bit, 1, 0), (y_bit, x_bit, 1, 0))
        spreads = [spread_of(order, core, total) for order in orders]
        chains = [Chain(gather_steps(shard, order, core, total)) for shard, order in zip(shards, orders)]
        small = Chain(gather_gains_steps(gains, x_bit, y_bit, core, total))
        both = [*chains, small]
        in_round(both)
        _, mlp_shard = in_round(both, beside=mlp_shard)
        bands = lax.all_gather(mlp_shard, AXES, axis=0)
        in_round(both)
        in_round(both)
        _, gain_rows = in_round(both, beside=small.result)
        *saved, first_sum, logs, weights = cross_forward(chains[0].result + chains[2].result, spreads[::2])
        *saved2, second_sum, logs2, weights2 = self_forward(chains[1].result + chains[3].result, spreads[1::2])
    else:
        every = lambda shard: lax.all_gather(shard.astype(LOW), AXES, axis=0, tiled=True).reshape(32, -1, shard.shape[1])
        inward = lambda m: jnp.concatenate([every(attn_in_t[3 * m + k]) for k in range(3)], axis=1)
        gain_rows = gather_gains(gains)
        lower = every(w_out_t)
        lift = lax.all_gather(w_in.astype(LOW), AXES, axis=1, tiled=True).T.reshape(32, -1, width)
        bands = jnp.concatenate([*jnp.split(lower, PARTS, axis=2), lift], axis=1)
        *saved, first_sum, logs, weights = cross_forward([inward(0), every(attn_out_t[0])], (None, None))
        *saved2, second_sum, logs2, weights2 = self_forward([inward(1), every(attn_out_t[1])], (None, None))

    normal, partial, hidden_grad0, *lower_grad0 = mlp_forward(
        0, second_sum, cot_rows, (gain_rows[3:],), bands, hidden, cut
    )

    def mlp_second():
        return mlp_forward(1, partial, cot_rows, (normal, flat(skip)), bands, hidden, cut)

    def mlp_back():
        return mlp_backward(
            gain_rows[3:], second_sum, cot_rows, normal, (hidden_grad0, hidden_grad1), bands, hidden, cut
        )

    def self_scores():
        return scores_grad(None, second_grad, (*saved2, logs2), weights2, images)

    def self_matrices():
        return matrix_grads(gain_rows, None, first_sum, second_grad, saved2[3], score_grads2, cut)

    def self_project():
        return project_grad(gain_rows, None, first_sum, second_grad, score_grads2, weights2)

    def cross_scores():
        return scores_grad(own_counts, first_grad, (*saved, logs), weights, images)

    def cross_matrices():
        return matrix_grads(gain_rows, pixel_rows, latent_rows, first_grad, saved[3], score_grads, cut)

    def cross_project():
        return project_grad(gain_rows, pixel_rows, latent_rows, first_grad, score_grads, weights)

    if fast:
        scatter = lambda blocks, last=False: Chain(scatter_steps(*blocks, x_bit, y_bit, core, total, last))
        live = [scatter(lower_grad0)]
        latents_out, hidden_grad1, *lower_grad1 = in_round(live, mlp_second)
        live.append(scatter(lower_grad1))
        second_grad, gain3_grad, *lift_grad = in_round(live, mlp_back)
        live.append(scatter(lift_grad))
        score_grads2 = in_round(live, self_scores)
        live.append(scatter(in_round(live, self_matrices, longer=live[2:])))
        (first_grad,), (gain2_grad,) = in_round(live, self_project)
        score_grads = in_round(live, cross_scores, longer=live[3:])
        blocks, score_grads = in_round(live, cross_matrices, beside=score_grads)
        live.append(scatter(blocks, True))
        (latents_grad, pixels_grad), (gain1_grad, gain0_grad) = in_round(live, cross_project)
        in_round(live, longer=live[4:])
        in_round(live)
        gains_grad = jnp.concatenate([gain0_grad, gain1_grad, gain2_grad, gain3_grad], axis=0)
        gains_sum = scatter_gains(gains_grad)
        while any(chain.wanted for chain in live):
            in_round(live)
        lower0, lower1, lift_sum, own, cross = [chain.result for chain in live]
        lower_sum = jnp.concatenate([*lower0, *lower1], axis=1)
        lift_sum = jnp.concatenate([*lift_sum], axis=0)
        sums, sums2 = [matrix_blocks(block, 4, attn_in.shape[2]) for block in (cross, own)]
    else:
        latents_out, hidden_grad1, lower_grad1 = mlp_second()
        second_grad, gain3_grad, lift_grad = mlp_back()
        score_grads2 = self_scores()
        grads2 = self_matrices()
        (first_grad,), (gain2_grad,) = self_project()
        score_grads = cross_scores()
        grads = cross_matrices()
        (latents_grad, pixels_grad), (gain1_grad, gain0_grad) = cross_project()
        gains_grad = jnp.concatenate([gain0_grad, gain1_grad, gain2_grad, gain3_grad], axis=0)
        gains_sum = scatter_gains(gains_grad)
        sum_of = lambda grad, along: lax.psum_scatter(grad, AXES, scatter_dimension=along, tiled=True)
        sums = [sum_of(g, 0) for g in grads]
        sums2 = [sum_of(g, 0) for g in grads2]
        lift_sum = sum_of(lift_grad, 1)
        lower_sum = sum_of(jnp.concatenate([*lower_grad0, lower_grad1], axis=1), 0)
    mixing_sum = jnp.swapaxes(jnp.stack([*sums[:3], *sums2[:3]]), 1, 2).astype(F32)
    outward_sum = jnp.swapaxes(jnp.stack([sums[3], sums2[3]]), 1, 2).astype(F32)
    mix = adamw(attn_in, mixing_sum, attn_in_first, attn_in_second, 0.05, 0.1)
    out = adamw(attn_out, outward_sum, attn_out_first, attn_out_second, 0.3, 0.1)
    lift_new = adamw(w_in, lift_sum.astype(F32), w_in_first, w_in_second, 0.05, 0.1)
    lower_new = adamw(w_out, lower_sum.T.astype(F32), w_out_first, w_out_second, 0.03, 0.1)
    gain_first, gain_second, gain_new = adamw(
        gains, gains_sum, gains_first, gains_second, 0.4, 0.0
    )
    return (
        whole(latents_out),
        whole(pixels_grad),
        whole(latents_grad),
        *mix,
        *out,
        *lift_new,
        *lower_new,
        gain_first,
        gain_second[:3],
        gain_second[3],
        gain_new,
    )


def solution(mesh):
    return jax.shard_map(
        local,
        mesh=mesh,
        in_specs=(
            P(("grp", "hd"), None, None),
            P(("grp", "hd"), None, None),
            P(("grp", "hd"), None, None),
            P("grp"),
            P(("grp", "hd"), None, None),
            P(None, None, ("grp", "hd")),
            P(None, None, ("grp", "hd")),
            P(None, ("grp", "hd")),
            P(None, ("grp", "hd")),
            P(None, ("grp", "hd")),
            P(None, None, ("grp", "hd")),
            P(None, None, ("grp", "hd")),
            P(None, None, ("grp", "hd")),
            P(None, None, ("grp", "hd")),
            P(None, ("grp", "hd")),
            P(None, ("grp", "hd")),
            P(None, ("grp", "hd")),
            P(None, ("grp", "hd")),
            P(None, ("grp", "hd")),
            P(None, ("grp", "hd")),
        ),
        out_specs=(
            P(("grp", "hd"), None, None),
            P(("grp", "hd"), None, None),
            P(("grp", "hd"), None, None),
            P(None, None, ("grp", "hd")),
            P(None, None, ("grp", "hd")),
            P(None, None, ("grp", "hd")),
            P(None, None, ("grp", "hd")),
            P(None, None, ("grp", "hd")),
            P(None, None, ("grp", "hd")),
            P(None, ("grp", "hd")),
            P(None, ("grp", "hd")),
            P(None, ("grp", "hd")),
            P(None, ("grp", "hd")),
            P(None, ("grp", "hd")),
            P(None, ("grp", "hd")),
            P(None, ("grp", "hd")),
            P(None, ("grp", "hd")),
            P(("grp", "hd")),
            P(None, ("grp", "hd")),
        ),
        check_vma=False,
    )
```

profile of v0, /device:TPU:0, one launch (start us, length us, event | category | flops | bytes accessed | tf_op | source)
XLA Modules:
  0.0 490.1 jit_solution(2909248800089062696)
XLA Ops:
  12.6 4.1 collective-permute-start
  16.8 1.7 collective-permute-start.2
  18.5 1.5 collective-permute-start.3
  20.7 3.0 collective-permute-done.4
  24.2 3.0 collective-permute-done.5
  27.4 4.2 collective-permute-done.6
  31.7 2.6 collective-permute-done.1
  36.5 1.6 collective-permute-start.9
  38.1 1.6 collective-permute-start.10
  39.7 2.1 collective-permute-start.11
  41.8 10.3 %collective-permute-done.11 = bf16[4,128]{1,0:T(4,128)(2,1)S(1)} collective-permute-done((bf16[4,128]{1,0:T(4,128)(2,1)S(1)}, bf16[4,128]{1,0:T(4,128)(2,1)S(1)}, u32[]{:S(2)}, u32[]{:S(2)}) %collective-permute-start.11) | collective-permute-done | bytes 1056 | tf_op jit(solution)/shard_map/ppermute | solution.py:42
  56.3 1.5 collective-permute-start.13
  60.0 3.3 collective-permute-start.14
  63.3 1.7 pad_maximum_fusion.11
  66.4 3.0 collective-permute-start.16
  70.9 9.1 %collective-permute-done.16 = bf16[8,128]{1,0:T(8,128)(2,1)S(1)} collective-permute-done((bf16[8,128]{1,0:T(8,128)(2,1)S(1)}, bf16[8,128]{1,0:T(8,128)(2,1)S(1)}, u32[]{:S(2)}, u32[]{:S(2)}) %collective-permute-start.16) | collective-permute-done | bytes 2080 | tf_op jit(solution)/shard_map/ppermute | solution.py:42
  80.1 13.2 %collective-permute-done.14 = bf16[4,32,1024]{2,1,0:T(8,128)(2,1)} collective-permute-done((bf16[4,32,1024]{2,1,0:T(8,128)(2,1)}, bf16[4,32,1024]{2,1,0:T(8,128)(2,1)}, u32[]{:S(2)}, u32[]{:S(2)}) %collective-permute-start.14) | collective-permute-done | bytes 262176 | tf_op jit(solution)/shard_map/ppermute | solution.py:42
  93.3 3.8 collective-permute-done.15
  103.5 20.9 %collective-permute-done.20.refs_9_ = bf16[8,32,1024]{2,1,0:T(8,128)(2,1)S(1)} collective-permute-done((bf16[8,32,1024]{2,1,0:T(8,128)(2,1)S(1)}, bf16[8,32,1024]{2,1,0:T(8,128)(2,1)S(1)}, u32[]{:S(2)}, u32[]{:S(2)}) %collective-permute-start.20) | collective-permute-done | bytes 524320 | tf_op jit(solution)/shard_map/ppermute | solution.py:42
  124.4 19.3 %collective-permute-done.21.refs_7_ = bf16[8,32,1024]{2,1,0:T(8,128)(2,1)S(1)} collective-permute-done((bf16[8,32,1024]{2,1,0:T(8,128)(2,1)S(1)}, bf16[8,32,1024]{2,1,0:T(8,128)(2,1)S(1)}, u32[]{:S(2)}, u32[]{:S(2)}) %collective-permute-start.21) | collective-permute-done | bytes 524320 | tf_op jit(solution)/shard_map/ppermute | solution.py:42
  143.7 3.7 collective-permute-done.19.refs_3_
  148.0 3.4 collective-permute-done.28.refs_8_
  153.2 3.2 collective-permute-done.27.refs_11_
  157.3 3.0 collective-permute-done.25.refs_5_
  160.8 18.5 %shard_map.349 = (bf16[768,1024]{1,0:T(8,128)(2,1)S(1)}, bf16[768,1024]{1,0:T(8,128)(2,1)S(1)}, bf16[768,1024]{1,0:T(8,128)(2,1)}, bf16[768,1024]{1,0:T(8,128)(2...) custom-call(s32[3]{0:T(128)S(1)} %dynamic_slice.3.refs_0_, ...), custom_call_target="tpu_custom_call" | custom-call | flops 7247757312 | bytes 17825792 | tf_op jit(solution)/shard_map/pallas_call | solution.py:364
  181.7 18.2 %shard_map.350 = (bf16[768,1024]{1,0:T(8,128)(2,1)S(1)}, bf16[768,1024]{1,0:T(8,128)(2,1)S(1)}, bf16[768,1024]{1,0:T(8,128)(2,1)}, bf16[768,1024]{1,0:T(8,128)(2...) custom-call(f32[4,1024]{1,0:T(4,128)S(1)} %reshape.238.refs_1_.refs_0_, ...), custom_call_target="tpu_custom_call" | custom-call | flops 7247757312 | bytes 17825792 | tf_op jit(solution)/shard_map/pallas_call | solution.py:364
  202.2 20.4 %shard_map.351 = (bf16[768,1024]{1,0:T(8,128)(2,1)}, f32[768,1024]{1,0:T(8,128)}, bf16[768,2048]{1,0:T(8,128)(2,1)}, bf16[2,16,32,1024]{3,2,1,0:T(8,128)(2,1)}, bf16[2,16,32,1024]{3,2,1,0:T(8,128)(2,1)}) custom-call(f32[768,1024]{1,0:T(8,128)} %get-tuple-element.195.second, bf16[768,1024]{1,0:T(8,128)(2,1)} %bitcast.227, f32[1,1024]{1,0:T(1,128)} %slice.346.refs_0_.gain_row, ...), custom_call_target="tpu_custom_call" | custom-call | flops 12884901888 | bytes 25165824 | tf_op jit(solution)/shard_map/pallas_call | solution.py:714
  222.7 18.9 %shard_map.352 = (bf16[768,1024]{1,0:T(8,128)(2,1)}, bf16[768,2048]{1,0:T(8,128)(2,1)}, bf16[2,16,32,1024]{3,2,1,0:T(8,128)(2,1)}, bf16[2,16,32,1024]{3,2,1,0:T(8,128)(2,1)}) custom-call(f32[768,1024]{1,0:T(8,128)} %get-tuple-element.198.second, bf16[768,1024]{1,0:T(8,128)(2,1)} %bitcast.228, bf16[768,1024]{1,0:T(8,128)(2,1)} %get-tuple-element.199.refs_0_.normal, ...), custom_call_target="tpu_custom_call" | custom-call | flops 12884901888 | bytes 25165824 | tf_op jit(solution)/shard_map/pallas_call | solution.py:714
  243.1 1.5 collective-permute-start.31
  244.7 20.3 %shard_map.353 = (f32[768,1024]{1,0:T(8,128)}, f32[1,1024]{1,0:T(1,128)}, bf16[2,16,512,128]{3,2,1,0:T(8,128)(2,1)}, bf16[2,16,512,128]{3,2,1,0:T(8,128)(2,1)}) custom-call(f32[1,1024]{1,0:T(1,128)} %slice.346.refs_0_.gain_row, f32[768,1024]{1,0:T(8,128)} %get-tuple-element.195.second, bf16[768,1024]{1,0:T(8,128)(2,1)} %bitcast.229, ...), custom_call_target="tpu_custom_call" | custom-call | flops 12884901888 | bytes 32505856 | tf_op jit(solution)/shard_map/pallas_call | solution.py:812
  265.8 2.1 collective-permute-start.34
  267.9 3.2 add_convert_fusion.20
  273.4 13.2 %shard_map.354 = (bf16[768,1024]{1,0:T(8,128)(2,1)S(1)}, bf16[768,1024]{1,0:T(8,128)(2,1)S(1)}, bf16[768,1024]{1,0:T(8,128)(2,1)S(1)}) custom-call(f32[768,1024]{1,0:T(8,128)} %get-tuple-element.220.refs_0_.refs_2_, bf16[768,1024]{1,0:T(8,128)(2,1)} %copy-done.7, bf16[768,1024]{1,0:T(8,128)(2,1)} %copy-done.8, bf16[768,1024]{1,0:T(8,128)(2,1)} %get-tuple-element.223.refs_3_, ...), custom_call_target="tpu_custom_call" | custom-call | flops 3623878656 | bytes 18350080 | tf_op jit(solution)/shard_map/pallas_call | solution.py:430
  287.8 3.2 collective-permute-done.35
  292.5 1.6 collective-permute-start.39
  295.3 11.4 %shard_map.355 = (bf16[2,16,64,1024]{3,2,1,0:T(8,128)(2,1)}, bf16[2,16,64,1024]{3,2,1,0:T(8,128)(2,1)}) custom-call(f32[4,1024]{1,0:T(4,128)S(1)} %reshape.238.refs_1_.refs_0_, f32[768,1024]{1,0:T(8,128)} %get-tuple-element.190.refs_1_, f32[768,1024]{1,0:T(8,128)} %get-tuple-element.220.refs_0_.refs_2_, bf16[768,1024]{1,0:T(8,128)(2,1)S(1)} %copy-done.6, ...), custom_call_target="tpu_custom_call" | custom-call | flops 6442450944 | bytes 20971520 | tf_op jit(solution)/shard_map/pallas_call | solution.py:522
  307.4 2.8 add_convert_fusion.8
  310.2 1.5 collective-permute-start.44
  311.8 1.7 collective-permute-start.45
  313.5 2.5 collective-permute-start.42
  316.4 12.0 %shard_map.356 = (f32[768,1024]{1,0:T(8,128)}, f32[1,1024]{1,0:T(1,128)S(1)}) custom-call(f32[4,1024]{1,0:T(4,128)S(1)} %reshape.238.refs_1_.refs_0_, f32[768,1024]{1,0:T(8,128)} %get-tuple-element.190.refs_1_, f32[768,1024]{1,0:T(8,128)} %get-tuple-element.220.refs_0_.refs_2_, bf16[768,1024]{1,0:T(8,128)(2,1)S(1)} %get-tuple-element.235.refs_4_.refs_3_, ...), custom_call_target="tpu_custom_call" | custom-call | flops 4831838208 | bytes 22020096 | tf_op jit(solution)/shard_map/pallas_call | solution.py:599
  328.4 7.5 %collective-permute-done.44 = bf16[8,512,128]{2,1,0:T(8,128)(2,1)S(1)} collective-permute-done((bf16[8,512,128]{2,1,0:T(8,128)(2,1)S(1)}, bf16[8,512,128]{2,1,0:T(8,128)(2,1)S(1)}, u32[]{:S(2)}, u32[]{:S(2)}) %collective-permute-start.44) | collective-permute-done | bytes 1048608 | tf_op jit(solution)/shard_map/ppermute | solution.py:42
  337.2 2.5 collective-permute-start.47
  339.8 1.7 collective-permute-start.48
  342.3 3.5 add_convert_fusion.4
  345.8 1.5 collective-permute-start.51
  347.7 13.9 %shard_map.357 = (bf16[768,1024]{1,0:T(8,128)(2,1)S(1)}, bf16[768,1024]{1,0:T(8,128)(2,1)S(1)}, bf16[768,1024]{1,0:T(8,128)(2,1)S(1)}) custom-call(s32[3]{0:T(128)S(1)} %dynamic_slice.3.refs_0_, f32[768,1024]{1,0:T(8,128)} %get-tuple-element.249.refs_1_.refs_3_, bf16[768,1024]{1,0:T(8,128)(2,1)} %copy-done.12, bf16[768,1024]{1,0:T(8,128)(2,1)} %copy-done.13, ...), custom_call_target="tpu_custom_call" | custom-call | flops 3623878656 | bytes 18350080 | tf_op jit(solution)/shard_map/pallas_call | solution.py:430
  364.0 1.8 fusion.26
  367.9 11.0 %shard_map.358 = (bf16[2,16,64,1024]{3,2,1,0:T(8,128)(2,1)}, bf16[2,16,64,1024]{3,2,1,0:T(8,128)(2,1)}) custom-call(f32[4,1024]{1,0:T(4,128)S(1)} %reshape.238.refs_1_.refs_0_, bf16[768,1024]{1,0:T(8,128)(2,1)S(1)} %bitcast.212, bf16[768,1024]{1,0:T(8,128)(2,1)S(1)} %bitcast.215, f32[768,1024]{1,0:T(8,128)} %get-tuple-element.249.refs_1_.refs_3_, ...), custom_call_target="tpu_custom_call" | custom-call | flops 6442450944 | bytes 20971520 | tf_op jit(solution)/shard_map/pallas_call | solution.py:522
  380.6 1.7 collective-permute-start.54
  385.2 10.6 %shard_map.359 = (f32[768,1024]{1,0:T(8,128)}, f32[768,1024]{1,0:T(8,128)}, f32[1,1024]{1,0:T(1,128)S(1)}, f32[1,1024]{1,0:T(1,128)S(1)}) custom-call(f32[4,1024]{1,0:T(4,128)S(1)} %reshape.238.refs_1_.refs_0_, bf16[768,1024]{1,0:T(8,128)(2,1)S(1)} %bitcast.213, bf16[768,1024]{1,0:T(8,128)(2,1)S(1)} %bitcast.216, ...), custom_call_target="tpu_custom_call" | custom-call | flops 4831838208 | bytes 22020096 | tf_op jit(solution)/shard_map/pallas_call | solution.py:599
  395.8 3.5 collective-permute-done.53
  402.3 2.0 add_convert_fusion
  404.3 1.5 collective-permute-start.59
  407.1 8.3 %collective-permute-done.57 = bf16[2,2,64,1024]{3,2,0,1:T(8,128)(2,1)S(1)} collective-permute-done((bf16[2,2,64,1024]{3,2,0,1:T(8,128)(2,1)S(1)}, bf16[2,2,64,1024]{3,2,0,1:T(8,128)(2,1)S(1)}, u32[]{:S(2)}, u32[]{:S(2)}) %collective-permute-start.57) | collective-permute-done | bytes 524320 | tf_op jit(solution)/shard_map/ppermute | solution.py:42
  416.2 12.6 %collective-permute-done.58 = bf16[1,2,64,1024]{3,2,0,1:T(8,128)(2,1)S(1)} collective-permute-done((bf16[1,2,64,1024]{3,2,0,1:T(8,128)(2,1)S(1)}, bf16[1,2,64,1024]{3,2,0,1:T(8,128)(2,1)S(1)}, u32[]{:S(2)}, u32[]{:S(2)}) %collective-permute-start.58) | collective-permute-done | bytes 262176 | tf_op jit(solution)/shard_map/ppermute | solution.py:42
  435.7 4.0 all-to-all-start.1
  439.7 2.1 fusion.57
  441.8 3.2 collective-permute-done.61
  450.1 3.6 all-to-all-start
  453.9 2.6 multiply_subtract_fusion.2
  457.9 20.3 %all-to-all-done = bf16[4,2,64,1024]{3,2,1,0:T(8,128)(2,1)S(1)} async-done(((bf16[4,2,64,1024]{3,2,1,0:T(8,128)(2,1)}), bf16[4,2,64,1024]{3,2,1,0:T(8,128)(2,1)S(1)}, u32[]{:S(2)}, u32[]{:S(2)}) %all-to-all-start) | async-done | bytes 1048608 | tf_op jit(solution)/shard_map/all_to_all | solution.py:113
  479.2 1.9 multiply_subtract_fusion.3
  481.2 1.8 multiply_subtract_fusion
  (327 shorter events, 73.8 us)
Async XLA Ops:
  7.2 195.0 %all-gather.3.cloned.1.call-start = ((), (), s32[]{:S(2)}) async-start(), calls=%async_computation.2 | async-start | bytes 17301504 | tf_op jit(solution)/shard_map/all_gather | solution.py:888
  12.6 19.1 %collective-permute-start = (bf16[1,96,1024]{2,1,0:T(8,128)(2,1)S(1)}, bf16[1,96,1024]{2,1,0:T(8,128)(2,1)S(1)}, u32[]{:S(2)}, u32[]{:S(2)}) collective-permute-start(bf16[1,96,1024]{2,1,0:T(8,128)(2,1)S(1)} %get-tuple-element.158), channel_id=1, source_target_pairs={{0,2},{1,3},{2,0},{3,1},{4,6},{5,7},{6,4},{7,5},{8,10},{9,11},{10,... | collective-permute-start | bytes 589832 | tf_op jit(solution)/shard_map/ppermute | solution.py:42
  16.7 17.5 %collective-permute-start.1 = (bf16[1,96,1024]{2,1,0:T(8,128)(2,1)S(1)}, bf16[1,96,1024]{2,1,0:T(8,128)(2,1)S(1)}, u32[]{:S(2)}, u32[]{:S(2)}) collective-permute-start(bf16[1,96,1024]{2,1,0:T(8,128)(2,1)S(1)} %get-tuple-element.159), channel_id=1, source_target_pairs={{0,2},{1,3},{2,0},{3,1},{4,6},{5,7},{6,4},{7,5},{8,10},{9,11},{10,... | collective-permute-start | bytes 589832 | tf_op jit(solution)/shard_map/ppermute | solution.py:42
  16.8 14.9 %collective-permute-start.2 = (bf16[1,32,1024]{2,1,0:T(8,128)(2,1)S(1)}, bf16[1,32,1024]{2,1,0:T(8,128)(2,1)S(1)}, u32[]{:S(2)}, u32[]{:S(2)}) collective-permute-start(bf16[1,32,1024]{2,1,0:T(8,128)(2,1)S(1)} %get-tuple-element.160), channel_id=1, source_target_pairs={{0,8},{1,9},{2,10},{3,11},{4,12},{5,13},{6,14},{7,15},{8,0},{9,1},... | collective-permute-start | bytes 196616 | tf_op jit(solution)/shard_map/ppermute | solution.py:42
  18.5 13.1 %collective-permute-start.3 = (bf16[1,32,1024]{2,1,0:T(8,128)(2,1)S(1)}, bf16[1,32,1024]{2,1,0:T(8,128)(2,1)S(1)}, u32[]{:S(2)}, u32[]{:S(2)}) collective-permute-start(bf16[1,32,1024]{2,1,0:T(8,128)(2,1)S(1)} %get-tuple-element.161), channel_id=1, source_target_pairs={{0,16},{1,17},{2,18},{3,19},{4,20},{5,21},{6,22},{7,23},{8,24},{9,... | collective-permute-start | bytes 196616 | tf_op jit(solution)/shard_map/ppermute | solution.py:42
  20.1 3.5 collective-permute-start.4
  23.7 3.5 collective-permute-start.5
  27.2 4.4 collective-permute-start.6
  34.3 17.8 %collective-permute-start.7 = (bf16[2,96,1024]{2,1,0:T(8,128)(2,1)S(1)}, bf16[2,96,1024]{2,1,0:T(8,128)(2,1)S(1)}, u32[]{:S(2)}, u32[]{:S(2)}) collective-permute-start(bf16[2,96,1024]{2,1,0:T(8,128)(2,1)S(1)} %pad_maximum_fusion.6), channel_id=1, source_target_pairs={{0,1},{1,0},{2,3},{3,2},{4,5},{5,4},{6,7},{7,6},{8,9},{9,8},{10,11... | collective-permute-start | bytes 1179656 | tf_op jit(solution)/shard_map/ppermute | solution.py:42
  35.1 18.0 %collective-permute-start.8 = (bf16[2,96,1024]{2,1,0:T(8,128)(2,1)S(1)}, bf16[2,96,1024]{2,1,0:T(8,128)(2,1)S(1)}, u32[]{:S(2)}, u32[]{:S(2)}) collective-permute-start(bf16[2,96,1024]{2,1,0:T(8,128)(2,1)S(1)} %pad_maximum_fusion.7), channel_id=1, source_target_pairs={{0,1},{1,0},{2,3},{3,2},{4,5},{5,4},{6,7},{7,6},{8,9},{9,8},{10,11... | collective-permute-start | bytes 1179656 | tf_op jit(solution)/shard_map/ppermute | solution.py:42
  36.5 15.6 %collective-permute-start.9 = (bf16[2,32,1024]{2,1,0:T(8,128)(2,1)S(1)}, bf16[2,32,1024]{2,1,0:T(8,128)(2,1)S(1)}, u32[]{:S(2)}, u32[]{:S(2)}) collective-permute-start(bf16[2,32,1024]{2,1,0:T(8,128)(2,1)S(1)} %pad_maximum_fusion.12), channel_id=1, source_target_pairs={{0,16},{1,17},{2,18},{3,19},{4,20},{5,21},{6,22},{7,23},{8,24},{9,... | collective-permute-start | bytes 393224 | tf_op jit(solution)/shard_map/ppermute | solution.py:42
  38.1 13.9 %collective-permute-start.10 = (bf16[2,32,1024]{2,1,0:T(8,128)(2,1)S(1)}, bf16[2,32,1024]{2,1,0:T(8,128)(2,1)S(1)}, u32[]{:S(2)}, u32[]{:S(2)}) collective-permute-start(bf16[2,32,1024]{2,1,0:T(8,128)(2,1)S(1)} %pad_maximum_fusion.13), channel_id=1, source_target_pairs={{0,8},{1,9},{2,10},{3,11},{4,12},{5,13},{6,14},{7,15},{8,0},{9,1},... | collective-permute-start | bytes 393224 | tf_op jit(solution)/shard_map/ppermute | solution.py:42
  39.7 12.4 %collective-permute-start.11 = (bf16[4,128]{1,0:T(4,128)(2,1)S(1)}, bf16[4,128]{1,0:T(4,128)(2,1)S(1)}, u32[]{:S(2)}, u32[]{:S(2)}) collective-permute-start(bf16[4,128]{1,0:T(4,128)(2,1)S(1)} %pad_maximum_fusion.15), channel_id=1, source_target_pairs={{0,2},{1,3},{2,0},{3,1},{4,6},{5,7},{6,4},{7,5},{8,10},{9,11},{10,... | collective-permute-start | bytes 3080 | tf_op jit(solution)/shard_map/ppermute | solution.py:42
  54.1 42.9 %collective-permute-start.12 = (bf16[4,96,1024]{2,1,0:T(8,128)(2,1)}, bf16[4,96,1024]{2,1,0:T(8,128)(2,1)S(1)}, u32[]{:S(2)}, u32[]{:S(2)}) collective-permute-start(bf16[4,96,1024]{2,1,0:T(8,128)(2,1)} %pad_maximum_fusion.1), channel_id=1, source_target_pairs={{0,8},{1,9},{2,10},{3,11},{4,12},{5,13},{6,14},{7,15},{8,0},{9,1},... | collective-permute-start | bytes 2359304 | tf_op jit(solution)/shard_map/ppermute | solution.py:42
  56.3 40.7 %collective-permute-start.13 = (bf16[4,96,1024]{2,1,0:T(8,128)(2,1)}, bf16[4,96,1024]{2,1,0:T(8,128)(2,1)S(1)}, u32[]{:S(2)}, u32[]{:S(2)}) collective-permute-start(bf16[4,96,1024]{2,1,0:T(8,128)(2,1)} %pad_maximum_fusion.2), channel_id=1, source_target_pairs={{0,16},{1,17},{2,18},{3,19},{4,20},{5,21},{6,22},{7,23},{8,24},{9,... | collective-permute-start | bytes 2359304 | tf_op jit(solution)/shard_map/ppermute | solution.py:42
  60.0 33.3 %collective-permute-start.14 = (bf16[4,32,1024]{2,1,0:T(8,128)(2,1)}, bf16[4,32,1024]{2,1,0:T(8,128)(2,1)}, u32[]{:S(2)}, u32[]{:S(2)}) collective-permute-start(bf16[4,32,1024]{2,1,0:T(8,128)(2,1)} %pad_maximum_fusion.10), channel_id=1, source_target_pairs={{0,2},{1,3},{2,0},{3,1},{4,6},{5,7},{6,4},{7,5},{8,10},{9,11},{10,... | collective-permute-start | bytes 786440 | tf_op jit(solution)/shard_map/ppermute | solution.py:42
  65.0 32.0 %collective-permute-start.15 = (bf16[4,32,1024]{2,1,0:T(8,128)(2,1)}, bf16[4,32,1024]{2,1,0:T(8,128)(2,1)S(1)}, u32[]{:S(2)}, u32[]{:S(2)}) collective-permute-start(bf16[4,32,1024]{2,1,0:T(8,128)(2,1)} %pad_maximum_fusion.11), channel_id=1, source_target_pairs={{0,2},{1,3},{2,0},{3,1},{4,6},{5,7},{6,4},{7,5},{8,10},{9,11},{10,... | collective-permute-start | bytes 786440 | tf_op jit(solution)/shard_map/ppermute | solution.py:42
  66.4 13.7 %collective-permute-start.16 = (bf16[8,128]{1,0:T(8,128)(2,1)S(1)}, bf16[8,128]{1,0:T(8,128)(2,1)S(1)}, u32[]{:S(2)}, u32[]{:S(2)}) collective-permute-start(bf16[8,128]{1,0:T(8,128)(2,1)S(1)} %concatenate.77), channel_id=1, source_target_pairs={{0,1},{1,0},{2,3},{3,2},{4,5},{5,4},{6,7},{7,6},{8,9},{9,8},{10,11... | collective-permute-start | bytes 6152 | tf_op jit(solution)/shard_map/ppermute | solution.py:42
  98.0 45.8 %collective-permute-start.18 = (bf16[8,96,1024]{2,1,0:T(8,128)(2,1)}, bf16[8,96,1024]{2,1,0:T(8,128)(2,1)}, u32[]{:S(2)}, u32[]{:S(2)}) collective-permute-start(bf16[8,96,1024]{2,1,0:T(8,128)(2,1)} %constant_dynamic-update-slice_fusion.refs_4_), channel_id=1, source_target_pairs={{0,16},{1,17},{2,18},{3,19},{4,20},{5,21},{6,22},{7,23},{8,24},{9,... | collective-permute-start | bytes 4718600 | tf_op jit(solution)/shard_map/ppermute | solution.py:42
  99.4 48.1 %collective-permute-start.19 = (bf16[8,96,1024]{2,1,0:T(8,128)(2,1)}, bf16[8,96,1024]{2,1,0:T(8,128)(2,1)}, u32[]{:S(2)}, u32[]{:S(2)}) collective-permute-start(bf16[8,96,1024]{2,1,0:T(8,128)(2,1)} %constant_dynamic-update-slice_fusion.4.refs_2_), channel_id=1, source_target_pairs={{0,8},{1,9},{2,10},{3,11},{4,12},{5,13},{6,14},{7,15},{8,0},{9,1},... | collective-permute-start | bytes 4718600 | tf_op jit(solution)/shard_map/ppermute | solution.py:42
  101.0 23.4 %collective-permute-start.20 = (bf16[8,32,1024]{2,1,0:T(8,128)(2,1)S(1)}, bf16[8,32,1024]{2,1,0:T(8,128)(2,1)S(1)}, u32[]{:S(2)}, u32[]{:S(2)}) collective-permute-start(bf16[8,32,1024]{2,1,0:T(8,128)(2,1)S(1)} %constant_dynamic-update-slice_fusion.8.refs_8_), channel_id=1, source_target_pairs={{0,1},{1,0},{2,3},{3,2},{4,5},{5,4},{6,7},{7,6},{8,9},{9,8},{10,11... | collective-permute-start | bytes 1572872 | tf_op jit(solution)/shard_map/ppermute | solution.py:42
  102.0 41.7 %collective-permute-start.21 = (bf16[8,32,1024]{2,1,0:T(8,128)(2,1)S(1)}, bf16[8,32,1024]{2,1,0:T(8,128)(2,1)S(1)}, u32[]{:S(2)}, u32[]{:S(2)}) collective-permute-start(bf16[8,32,1024]{2,1,0:T(8,128)(2,1)S(1)} %constant_dynamic-update-slice_fusion.12.refs_6_), channel_id=1, source_target_pairs={{0,1},{1,0},{2,3},{3,2},{4,5},{5,4},{6,7},{7,6},{8,9},{9,8},{10,11... | collective-permute-start | bytes 1572872 | tf_op jit(solution)/shard_map/ppermute | solution.py:42
  103.3 49.1 %collective-permute-start.17 = (bf16[8,96,1024]{2,1,0:T(8,128)(2,1)}, bf16[8,96,1024]{2,1,0:T(8,128)(2,1)}, u32[]{:S(2)}, u32[]{:S(2)}) collective-permute-start(bf16[8,96,1024]{2,1,0:T(8,128)(2,1)} %constant_dynamic-update-slice_fusion.refs_4_), channel_id=1, source_target_pairs={{0,4},{1,5},{2,6},{3,7},{4,0},{5,1},{6,2},{7,3},{8,12},{9,13},{10,... | collective-permute-start | bytes 4718600 | tf_op jit(solution)/shard_map/ppermute | solution.py:42
  124.4 28.8 %collective-permute-start.24 = (bf16[8,96,1024]{2,1,0:T(8,128)(2,1)}, bf16[8,96,1024]{2,1,0:T(8,128)(2,1)}, u32[]{:S(2)}, u32[]{:S(2)}) collective-permute-start(bf16[8,96,1024]{2,1,0:T(8,128)(2,1)} %constant_dynamic-update-slice_fusion.4.refs_2_), channel_id=1, source_target_pairs={{0,4},{1,5},{2,6},{3,7},{4,0},{5,1},{6,2},{7,3},{8,12},{9,13},{10,... | collective-permute-start | bytes 4718600 | tf_op jit(solution)/shard_map/ppermute | solution.py:42
  143.7 4.3 collective-permute-start.26
  147.5 9.8 %collective-permute-start.23 = (bf16[8,96,1024]{2,1,0:T(8,128)(2,1)}, bf16[8,96,1024]{2,1,0:T(8,128)(2,1)}, u32[]{:S(2)}, u32[]{:S(2)}) collective-permute-start(bf16[8,96,1024]{2,1,0:T(8,128)(2,1)} %collective-permute-done.18.refs_5_), channel_id=1, source_target_pairs={{0,4},{1,5},{2,6},{3,7},{4,0},{5,1},{6,2},{7,3},{8,12},{9,13},{10,... | collective-permute-start | bytes 4718600 | tf_op jit(solution)/shard_map/ppermute | solution.py:42
  147.5 12.7 %collective-permute-start.25 = (bf16[8,96,1024]{2,1,0:T(8,128)(2,1)}, bf16[8,96,1024]{2,1,0:T(8,128)(2,1)}, u32[]{:S(2)}, u32[]{:S(2)}) collective-permute-start(bf16[8,96,1024]{2,1,0:T(8,128)(2,1)} %collective-permute-done.19.refs_3_), channel_id=1, source_target_pairs={{0,4},{1,5},{2,6},{3,7},{4,0},{5,1},{6,2},{7,3},{8,12},{9,13},{10,... | collective-permute-start | bytes 4718600 | tf_op jit(solution)/shard_map/ppermute | solution.py:42
  152.2 4.2 collective-permute-start.27
  152.3 4.1 collective-permute-start.29
  222.6 19.1 %collective-permute-start.30 = (bf16[2,16,32,1024]{3,2,1,0:T(8,128)(2,1)}, bf16[2,16,32,1024]{3,2,1,0:T(8,128)(2,1)S(1)}, u32[]{:S(2)}, u32[]{:S(2)}) collective-permute-start(bf16[2,16,32,1024]{3,2,1,0:T(8,128)(2,1)} %get-tuple-element.197), channel_id=1, source_target_pairs={{0,4},{1,5},{2,6},{3,7},{4,0},{5,1},{6,2},{7,3},{8,12},{9,13},{10,... | collective-permute-start | bytes 6291464 | tf_op jit(solution)/shard_map/ppermute | solution.py:42
  241.6 23.3 %collective-permute-start.33 = (bf16[2,16,32,1024]{3,2,1,0:T(8,128)(2,1)}, bf16[2,16,32,1024]{3,2,1,0:T(8,128)(2,1)}, u32[]{:S(2)}, u32[]{:S(2)}) collective-permute-start(bf16[2,16,32,1024]{3,2,1,0:T(8,128)(2,1)} %get-tuple-element.207), channel_id=1, source_target_pairs={{0,4},{1,5},{2,6},{3,7},{4,0},{5,1},{6,2},{7,3},{8,12},{9,13},{10,... | collective-permute-start | bytes 6291464 | tf_op jit(solution)/shard_map/ppermute | solution.py:42
  243.1 21.8 %collective-permute-start.31 = (bf16[8,32,1024]{2,1,0:T(8,128)(2,1)S(1)}, bf16[8,32,1024]{2,1,0:T(8,128)(2,1)S(1)}, u32[]{:S(2)}, u32[]{:S(2)}) collective-permute-start(bf16[8,32,1024]{2,1,0:T(8,128)(2,1)S(1)} %get-tuple-element.331), channel_id=1, source_target_pairs={{0,16},{1,17},{2,18},{3,19},{4,20},{5,21},{6,22},{7,23},{8,24},{9,... | collective-permute-start | bytes 1572872 | tf_op jit(solution)/shard_map/ppermute | solution.py:42
  244.7 20.3 %collective-permute-start.32 = (bf16[8,32,1024]{2,1,0:T(8,128)(2,1)S(1)}, bf16[8,32,1024]{2,1,0:T(8,128)(2,1)S(1)}, u32[]{:S(2)}, u32[]{:S(2)}) collective-permute-start(bf16[8,32,1024]{2,1,0:T(8,128)(2,1)S(1)} %get-tuple-element.330), channel_id=1, source_target_pairs={{0,8},{1,9},{2,10},{3,11},{4,12},{5,13},{6,14},{7,15},{8,0},{9,1},... | collective-permute-start | bytes 1572872 | tf_op jit(solution)/shard_map/ppermute | solution.py:42
  265.7 25.2 %collective-permute-start.38 = (bf16[2,16,512,128]{3,2,1,0:T(8,128)(2,1)}, bf16[2,16,512,128]{3,2,1,0:T(8,128)(2,1)S(1)}, u32[]{:S(2)}, u32[]{:S(2)}) collective-permute-start(bf16[2,16,512,128]{3,2,1,0:T(8,128)(2,1)} %get-tuple-element.219), channel_id=1, source_target_pairs={{0,4},{1,5},{2,6},{3,7},{4,0},{5,1},{6,2},{7,3},{8,12},{9,13},{10,... | collective-permute-start | bytes 12582920 | tf_op jit(solution)/shard_map/ppermute | solution.py:42
  265.8 21.9 %collective-permute-start.34 = (bf16[4,32,1024]{2,1,0:T(8,128)(2,1)S(1)}, bf16[4,32,1024]{2,1,0:T(8,128)(2,1)S(1)}, u32[]{:S(2)}, u32[]{:S(2)}) collective-permute-start(bf16[4,32,1024]{2,1,0:T(8,128)(2,1)S(1)} %fusion.40), channel_id=1, source_target_pairs={{0,8},{1,9},{2,10},{3,11},{4,12},{5,13},{6,14},{7,15},{8,0},{9,1},... | collective-permute-start | bytes 786440 | tf_op jit(solution)/shard_map/ppermute | solution.py:42
  271.1 19.8 %collective-permute-start.36 = (bf16[8,32,1024]{2,1,0:T(8,128)(2,1)S(1)}, bf16[8,32,1024]{2,1,0:T(8,128)(2,1)S(1)}, u32[]{:S(2)}, u32[]{:S(2)}) collective-permute-start(bf16[8,32,1024]{2,1,0:T(8,128)(2,1)S(1)} %get-tuple-element.327), channel_id=1, source_target_pairs={{0,16},{1,17},{2,18},{3,19},{4,20},{5,21},{6,22},{7,23},{8,24},{9,... | collective-permute-start | bytes 1572872 | tf_op jit(solution)/shard_map/ppermute | solution.py:42
  271.7 19.2 %collective-permute-start.37 = (bf16[8,32,1024]{2,1,0:T(8,128)(2,1)S(1)}, bf16[8,32,1024]{2,1,0:T(8,128)(2,1)S(1)}, u32[]{:S(2)}, u32[]{:S(2)}) collective-permute-start(bf16[8,32,1024]{2,1,0:T(8,128)(2,1)S(1)} %get-tuple-element.326), channel_id=1, source_target_pairs={{0,8},{1,9},{2,10},{3,11},{4,12},{5,13},{6,14},{7,15},{8,0},{9,1},... | collective-permute-start | bytes 1572872 | tf_op jit(solution)/shard_map/ppermute | solution.py:42
  272.3 18.6 %collective-permute-start.35 = (bf16[4,32,1024]{2,1,0:T(8,128)(2,1)S(1)}, bf16[4,32,1024]{2,1,0:T(8,128)(2,1)}, u32[]{:S(2)}, u32[]{:S(2)}) collective-permute-start(bf16[4,32,1024]{2,1,0:T(8,128)(2,1)S(1)} %fusion.39), channel_id=1, source_target_pairs={{0,16},{1,17},{2,18},{3,19},{4,20},{5,21},{6,22},{7,23},{8,24},{9,... | collective-permute-start | bytes 786440 | tf_op jit(solution)/shard_map/ppermute | solution.py:42
  292.5 14.2 %collective-permute-start.39 = (bf16[2,2,32,1024]{3,2,1,0:T(8,128)(2,1)S(1)}, bf16[2,2,32,1024]{3,2,1,0:T(8,128)(2,1)S(1)}, u32[]{:S(2)}, u32[]{:S(2)}) collective-permute-start(bf16[2,2,32,1024]{3,2,1,0:T(8,128)(2,1)S(1)} %pad_maximum_fusion.9), channel_id=1, source_target_pairs={{0,1},{1,0},{2,3},{3,2},{4,5},{5,4},{6,7},{7,6},{8,9},{9,8},{10,11... | collective-permute-start | bytes 786440 | tf_op jit(solution)/shard_map/ppermute | solution.py:42
  294.2 12.6 %collective-permute-start.40 = (bf16[4,32,1024]{2,1,0:T(8,128)(2,1)S(1)}, bf16[4,32,1024]{2,1,0:T(8,128)(2,1)S(1)}, u32[]{:S(2)}, u32[]{:S(2)}) collective-permute-start(bf16[4,32,1024]{2,1,0:T(8,128)(2,1)S(1)} %fusion.36), channel_id=1, source_target_pairs={{0,8},{1,9},{2,10},{3,11},{4,12},{5,13},{6,14},{7,15},{8,0},{9,1},... | collective-permute-start | bytes 786440 | tf_op jit(solution)/shard_map/ppermute | solution.py:42
  294.7 12.1 %collective-permute-start.41 = (bf16[4,32,1024]{2,1,0:T(8,128)(2,1)S(1)}, bf16[4,32,1024]{2,1,0:T(8,128)(2,1)S(1)}, u32[]{:S(2)}, u32[]{:S(2)}) collective-permute-start(bf16[4,32,1024]{2,1,0:T(8,128)(2,1)S(1)} %fusion.35), channel_id=1, source_target_pairs={{0,16},{1,17},{2,18},{3,19},{4,20},{5,21},{6,22},{7,23},{8,24},{9,... | collective-permute-start | bytes 786440 | tf_op jit(solution)/shard_map/ppermute | solution.py:42
  307.4 29.6 %collective-permute-start.46 = (bf16[2,16,64,1024]{3,2,1,0:T(8,128)(2,1)}, bf16[2,16,64,1024]{3,2,1,0:T(8,128)(2,1)}, u32[]{:S(2)}, u32[]{:S(2)}) collective-permute-start(bf16[2,16,64,1024]{3,2,1,0:T(8,128)(2,1)} %get-tuple-element.243), channel_id=1, source_target_pairs={{0,4},{1,5},{2,6},{3,7},{4,0},{5,1},{6,2},{7,3},{8,12},{9,13},{10,... | collective-permute-start | bytes 12582920 | tf_op jit(solution)/shard_map/ppermute | solution.py:42
  310.2 25.6 %collective-permute-start.44 = (bf16[8,512,128]{2,1,0:T(8,128)(2,1)S(1)}, bf16[8,512,128]{2,1,0:T(8,128)(2,1)S(1)}, u32[]{:S(2)}, u32[]{:S(2)}) collective-permute-start(bf16[8,512,128]{2,1,0:T(8,128)(2,1)S(1)} %get-tuple-element.322), channel_id=1, source_target_pairs={{0,16},{1,17},{2,18},{3,19},{4,20},{5,21},{6,22},{7,23},{8,24},{9,... | collective-permute-start | bytes 3145736 | tf_op jit(solution)/shard_map/ppermute | solution.py:42
  311.8 25.3 %collective-permute-start.45 = (bf16[8,512,128]{2,1,0:T(8,128)(2,1)S(1)}, bf16[8,512,128]{2,1,0:T(8,128)(2,1)S(1)}, u32[]{:S(2)}, u32[]{:S(2)}) collective-permute-start(bf16[8,512,128]{2,1,0:T(8,128)(2,1)S(1)} %get-tuple-element.321), channel_id=1, source_target_pairs={{0,8},{1,9},{2,10},{3,11},{4,12},{5,13},{6,14},{7,15},{8,0},{9,1},... | collective-permute-start | bytes 3145736 | tf_op jit(solution)/shard_map/ppermute | solution.py:42
  313.5 14.8 %collective-permute-start.42 = (bf16[1,2,32,1024]{3,2,1,0:T(8,128)(2,1)S(1)}, bf16[1,2,32,1024]{3,2,1,0:T(8,128)(2,1)S(1)}, u32[]{:S(2)}, u32[]{:S(2)}) collective-permute-start(bf16[1,2,32,1024]{3,2,1,0:T(8,128)(2,1)S(1)} %slice.460), channel_id=1, source_target_pairs={{0,2},{1,3},{2,0},{3,1},{4,6},{5,7},{6,4},{7,5},{8,10},{9,11},{10,... | collective-permute-start | bytes 393224 | tf_op jit(solution)/shard_map/ppermute | solution.py:42
  316.3 12.1 %collective-permute-start.43 = (bf16[2,2,32,1024]{3,2,0,1:T(8,128)(2,1)S(1)}, bf16[2,2,32,1024]{3,2,0,1:T(8,128)(2,1)S(1)}, u32[]{:S(2)}, u32[]{:S(2)}) collective-permute-start(bf16[2,2,32,1024]{3,2,0,1:T(8,128)(2,1)S(1)} %fusion.49), channel_id=1, source_target_pairs={{0,1},{1,0},{2,3},{3,2},{4,5},{5,4},{6,7},{7,6},{8,9},{9,8},{10,11... | collective-permute-start | bytes 786440 | tf_op jit(solution)/shard_map/ppermute | solution.py:42
  337.2 26.8 %collective-permute-start.47 = (bf16[1,2,32,1024]{3,2,0,1:T(8,128)(2,1)S(1)}, bf16[1,2,32,1024]{3,2,0,1:T(8,128)(2,1)}, u32[]{:S(2)}, u32[]{:S(2)}) collective-permute-start(bf16[1,2,32,1024]{3,2,0,1:T(8,128)(2,1)S(1)} %slice.465), channel_id=1, source_target_pairs={{0,2},{1,3},{2,0},{3,1},{4,6},{5,7},{6,4},{7,5},{8,10},{9,11},{10,... | collective-permute-start | bytes 393224 | tf_op jit(solution)/shard_map/ppermute | solution.py:42
  339.8 24.2 %collective-permute-start.48 = (bf16[4,512,128]{2,1,0:T(8,128)(2,1)S(1)}, bf16[4,512,128]{2,1,0:T(8,128)(2,1)}, u32[]{:S(2)}, u32[]{:S(2)}) collective-permute-start(bf16[4,512,128]{2,1,0:T(8,128)(2,1)S(1)} %fusion.16), channel_id=1, source_target_pairs={{0,8},{1,9},{2,10},{3,11},{4,12},{5,13},{6,14},{7,15},{8,0},{9,1},... | collective-permute-start | bytes 1572872 | tf_op jit(solution)/shard_map/ppermute | solution.py:42
  341.7 22.3 %collective-permute-start.49 = (bf16[4,512,128]{2,1,0:T(8,128)(2,1)S(1)}, bf16[4,512,128]{2,1,0:T(8,128)(2,1)}, u32[]{:S(2)}, u32[]{:S(2)}) collective-permute-start(bf16[4,512,128]{2,1,0:T(8,128)(2,1)S(1)} %fusion.15), channel_id=1, source_target_pairs={{0,16},{1,17},{2,18},{3,19},{4,20},{5,21},{6,22},{7,23},{8,24},{9,... | collective-permute-start | bytes 1572872 | tf_op jit(solution)/shard_map/ppermute | solution.py:42
  345.8 33.5 %collective-permute-start.51 = (bf16[8,64,1024]{2,1,0:T(8,128)(2,1)S(1)}, bf16[8,64,1024]{2,1,0:T(8,128)(2,1)}, u32[]{:S(2)}, u32[]{:S(2)}) collective-permute-start(bf16[8,64,1024]{2,1,0:T(8,128)(2,1)S(1)} %get-tuple-element.319), channel_id=1, source_target_pairs={{0,16},{1,17},{2,18},{3,19},{4,20},{5,21},{6,22},{7,23},{8,24},{9,... | collective-permute-start | bytes 3145736 | tf_op jit(solution)/shard_map/ppermute | solution.py:42
  347.3 32.0 %collective-permute-start.52 = (bf16[8,64,1024]{2,1,0:T(8,128)(2,1)S(1)}, bf16[8,64,1024]{2,1,0:T(8,128)(2,1)}, u32[]{:S(2)}, u32[]{:S(2)}) collective-permute-start(bf16[8,64,1024]{2,1,0:T(8,128)(2,1)S(1)} %get-tuple-element.318), channel_id=1, source_target_pairs={{0,8},{1,9},{2,10},{3,11},{4,12},{5,13},{6,14},{7,15},{8,0},{9,1},... | collective-permute-start | bytes 3145736 | tf_op jit(solution)/shard_map/ppermute | solution.py:42
  367.4 11.9 %collective-permute-start.50 = (bf16[2,2,512,128]{3,2,0,1:T(8,128)(2,1)S(1)}, bf16[2,2,512,128]{3,2,0,1:T(8,128)(2,1)S(1)}, u32[]{:S(2)}, u32[]{:S(2)}) collective-permute-start(bf16[2,2,512,128]{3,2,0,1:T(8,128)(2,1)S(1)} %pad_maximum_fusion.4), channel_id=1, source_target_pairs={{0,1},{1,0},{2,3},{3,2},{4,5},{5,4},{6,7},{7,6},{8,9},{9,8},{10,11... | collective-permute-start | bytes 1572872 | tf_op jit(solution)/shard_map/ppermute | solution.py:42
  379.3 20.0 %collective-permute-start.56 = (bf16[2,16,64,1024]{3,2,1,0:T(8,128)(2,1)}, bf16[2,16,64,1024]{3,2,1,0:T(8,128)(2,1)S(1)}, u32[]{:S(2)}, u32[]{:S(2)}) collective-permute-start(bf16[2,16,64,1024]{3,2,1,0:T(8,128)(2,1)} %get-tuple-element.271), channel_id=1, source_target_pairs={{0,4},{1,5},{2,6},{3,7},{4,0},{5,1},{6,2},{7,3},{8,12},{9,13},{10,... | collective-permute-start | bytes 12582920 | tf_op jit(solution)/shard_map/ppermute | solution.py:42
  380.6 18.7 %collective-permute-start.54 = (bf16[4,64,1024]{2,1,0:T(8,128)(2,1)S(1)}, bf16[4,64,1024]{2,1,0:T(8,128)(2,1)S(1)}, u32[]{:S(2)}, u32[]{:S(2)}) collective-permute-start(bf16[4,64,1024]{2,1,0:T(8,128)(2,1)S(1)} %fusion.13), channel_id=1, source_target_pairs={{0,8},{1,9},{2,10},{3,11},{4,12},{5,13},{6,14},{7,15},{8,0},{9,1},... | collective-permute-start | bytes 1572872 | tf_op jit(solution)/shard_map/ppermute | solution.py:42
  383.7 15.6 %collective-permute-start.55 = (bf16[4,64,1024]{2,1,0:T(8,128)(2,1)S(1)}, bf16[4,64,1024]{2,1,0:T(8,128)(2,1)S(1)}, u32[]{:S(2)}, u32[]{:S(2)}) collective-permute-start(bf16[4,64,1024]{2,1,0:T(8,128)(2,1)S(1)} %fusion.12), channel_id=1, source_target_pairs={{0,16},{1,17},{2,18},{3,19},{4,20},{5,21},{6,22},{7,23},{8,24},{9,... | collective-permute-start | bytes 1572872 | tf_op jit(solution)/shard_map/ppermute | solution.py:42
  384.5 14.7 %collective-permute-start.53 = (bf16[1,2,512,128]{3,2,0,1:T(8,128)(2,1)S(1)}, bf16[1,2,512,128]{3,2,0,1:T(8,128)(2,1)S(1)}, u32[]{:S(2)}, u32[]{:S(2)}) collective-permute-start(bf16[1,2,512,128]{3,2,0,1:T(8,128)(2,1)S(1)} %slice.471), channel_id=1, source_target_pairs={{0,2},{1,3},{2,0},{3,1},{4,6},{5,7},{6,4},{7,5},{8,10},{9,11},{10,... | collective-permute-start | bytes 786440 | tf_op jit(solution)/shard_map/ppermute | solution.py:42
  402.2 13.2 %collective-permute-start.57 = (bf16[2,2,64,1024]{3,2,0,1:T(8,128)(2,1)S(1)}, bf16[2,2,64,1024]{3,2,0,1:T(8,128)(2,1)S(1)}, u32[]{:S(2)}, u32[]{:S(2)}) collective-permute-start(bf16[2,2,64,1024]{3,2,0,1:T(8,128)(2,1)S(1)} %pad_maximum_fusion.3), channel_id=1, source_target_pairs={{0,1},{1,0},{2,3},{3,2},{4,5},{5,4},{6,7},{7,6},{8,9},{9,8},{10,11... | collective-permute-start | bytes 1572872 | tf_op jit(solution)/shard_map/ppermute | solution.py:42
  404.3 24.5 %collective-permute-start.59 = (bf16[8,64,1024]{2,1,0:T(8,128)(2,1)S(1)}, bf16[8,64,1024]{2,1,0:T(8,128)(2,1)S(1)}, u32[]{:S(2)}, u32[]{:S(2)}) collective-permute-start(bf16[8,64,1024]{2,1,0:T(8,128)(2,1)S(1)} %get-tuple-element.314), channel_id=1, source_target_pairs={{0,16},{1,17},{2,18},{3,19},{4,20},{5,21},{6,22},{7,23},{8,24},{9,... | collective-permute-start | bytes 3145736 | tf_op jit(solution)/shard_map/ppermute | solution.py:42
  405.8 24.1 %collective-permute-start.60 = (bf16[8,64,1024]{2,1,0:T(8,128)(2,1)S(1)}, bf16[8,64,1024]{2,1,0:T(8,128)(2,1)S(1)}, u32[]{:S(2)}, u32[]{:S(2)}) collective-permute-start(bf16[8,64,1024]{2,1,0:T(8,128)(2,1)S(1)} %get-tuple-element.313), channel_id=1, source_target_pairs={{0,8},{1,9},{2,10},{3,11},{4,12},{5,13},{6,14},{7,15},{8,0},{9,1},... | collective-permute-start | bytes 3145736 | tf_op jit(solution)/shard_map/ppermute | solution.py:42
  415.7 13.2 %collective-permute-start.58 = (bf16[1,2,64,1024]{3,2,0,1:T(8,128)(2,1)S(1)}, bf16[1,2,64,1024]{3,2,0,1:T(8,128)(2,1)S(1)}, u32[]{:S(2)}, u32[]{:S(2)}) collective-permute-start(bf16[1,2,64,1024]{3,2,0,1:T(8,128)(2,1)S(1)} %slice.479), channel_id=1, source_target_pairs={{0,2},{1,3},{2,0},{3,1},{4,6},{5,7},{6,4},{7,5},{8,10},{9,11},{10,... | collective-permute-start | bytes 786440 | tf_op jit(solution)/shard_map/ppermute | solution.py:42
  431.0 13.9 %collective-permute-start.61 = (bf16[4,64,1024]{2,1,0:T(8,128)(2,1)}, bf16[4,64,1024]{2,1,0:T(8,128)(2,1)}, u32[]{:S(2)}, u32[]{:S(2)}) collective-permute-start(bf16[4,64,1024]{2,1,0:T(8,128)(2,1)} %fusion.8), channel_id=1, source_target_pairs={{0,8},{1,9},{2,10},{3,11},{4,12},{5,13},{6,14},{7,15},{8,0},{9,1},... | collective-permute-start | bytes 1572872 | tf_op jit(solution)/shard_map/ppermute | solution.py:42
  432.3 13.7 %collective-permute-start.62 = (bf16[4,64,1024]{2,1,0:T(8,128)(2,1)}, bf16[4,64,1024]{2,1,0:T(8,128)(2,1)}, u32[]{:S(2)}, u32[]{:S(2)}) collective-permute-start(bf16[4,64,1024]{2,1,0:T(8,128)(2,1)} %fusion.7), channel_id=1, source_target_pairs={{0,16},{1,17},{2,18},{3,19},{4,20},{5,21},{6,22},{7,23},{8,24},{9,... | collective-permute-start | bytes 1572872 | tf_op jit(solution)/shard_map/ppermute | solution.py:42
  435.7 14.4 %all-to-all-start.1 = ((f32[32,1,128]{2,1,0:T(1,128)}), f32[32,1,128]{2,1,0:T(1,128)S(1)}, u32[]{:S(2)}, u32[]{:S(2)}) async-start(f32[32,1,128]{2,1,0:T(1,128)} %bitcast.67), calls=%async_computation.1 | async-start | bytes 32768 | tf_op jit(solution)/shard_map/all_to_all | solution.py:228
  450.1 28.2 %all-to-all-start = ((bf16[4,2,64,1024]{3,2,1,0:T(8,128)(2,1)}), bf16[4,2,64,1024]{3,2,1,0:T(8,128)(2,1)S(1)}, u32[]{:S(2)}, u32[]{:S(2)}) async-start(bf16[4,2,64,1024]{3,2,1,0:T(8,128)(2,1)} %copy.51), calls=%async_computation | async-start | bytes 2097152 | tf_op jit(solution)/shard_map/all_to_all | solution.py:113
  (75 other events, 689.6 us)
Sparse Core Ops, SparseCore 0:
  53.2 148.1 all-gather.2
where the time goes:
time: 499 us; the launch traced here: 490 us
  Pallas kernels  169 us (34%)
  waiting for transfers between devices  166 us (33%)
  starting transfers between devices  65.9 us (13%)
  other arithmetic  45.2 us (9%)
  local copies, waits for them, and re-layouts  27.9 us (6%)
  between operations  15.5 us (3%)
    ppermute x60, waiting for transfers between devices, swap(): return lax.ppermute(block, AXES, [(j, j ^ 1 << bit) for j in range(total)])  135 us
    ppermute x60, starting transfers between devices, swap(): return lax.ppermute(block, AXES, [(j, j ^ 1 << bit) for j in range(total)])  57 us
    pallas_call x2, Pallas kernels, mlp_forward(): pl.pallas_call(functools.partial(mlp_forward_kernel, call, depth), out_sh...  39.3 us
    pallas_call x2, Pallas kernels, attend_block(): pl.pallas_call(functools.partial(attend_kernel, cross, images, rows // im...  36.7 us
    pallas_call x2, Pallas kernels, scores_grad(): pl.pallas_call(functools.partial(scores_grad_kernel, cross, images, rows...  27.1 us
    pallas_call x2, Pallas kernels, project_grad(): pl.pallas_call(functools.partial(project_grad_kernel, cross), out_shape=[...  22.5 us
    pallas_call x2, Pallas kernels, matrix_grads(): pl.pallas_call(functools.partial(matrix_grad_kernel, cross, depth), out_s...  22.4 us
    unnamed x156, local copies, waits for them, and re-layouts  20.5 us
  transfers between devices with their start and end apart: 66, of which 26 were waited for; matrix products, arithmetic and copies ran while one was open for 9% of the time, Pallas kernels for 30%

commit v1 on v0

--- a/solution.py
+++ b/solution.py
@@ -888,8 +888,10 @@
         bands = lax.all_gather(mlp_shard, AXES, axis=0)
         in_round(both)
         in_round(both)
-        _, gain_rows = in_round(both, beside=small.result)
-        *saved, first_sum, logs, weights = cross_forward(chains[0].result + chains[2].result, spreads[::2])
+        _, gain_rows = in_round(both, beside=small.result, longer=chains[1::2])
+        *saved, first_sum, logs, weights = in_round(
+            both, lambda: cross_forward(chains[0].result + chains[2].result, spreads[::2])
+        )
         *saved2, second_sum, logs2, weights2 = self_forward(chains[1].result + chains[3].result, spreads[1::2])
     else:
         every = lambda shard: lax.all_gather(shard.astype(LOW), AXES, axis=0, tiled=True).reshape(32, -1, shard.shape[1])

time: 499 us -> 499 us (level)
    ppermute x60, waiting for transfers between devices: 135 us -> 130 us  [swap(): return lax.ppermute(block, AXES, [(j, j ^ 1 << bit) for j in range(total)])]
    unnamed x156 -> x152, local copies, waits for them, and re-layouts: 20.5 us -> 20.8 us
  transfers between devices with their start and end apart: 66 -> 66, of which waited for: 26 -> 27; matrix products, arithmetic and copies ran while one was open for 9% -> 9% of each run, Pallas kernels for 30% -> 30%
where the time goes in v1:
time: 499 us; the launch traced here: 489 us
  Pallas kernels  170 us (34%)
  waiting for transfers between devices  163 us (33%)
  starting transfers between devices  67.5 us (14%)
  other arithmetic  45.2 us (9%)
  local copies, waits for them, and re-layouts  28.2 us (6%)
  between operations  15.5 us (3%)
    ppermute x60, waiting for transfers between devices, swap(): return lax.ppermute(block, AXES, [(j, j ^ 1 << bit) for j in range(total)])  130 us
    ppermute x60, starting transfers between devices, swap(): return lax.ppermute(block, AXES, [(j, j ^ 1 << bit) for j in range(total)])  59.8 us
    pallas_call x2, Pallas kernels, mlp_forward(): pl.pallas_call(functools.partial(mlp_forward_kernel, call, depth), out_sh...  39.3 us
    pallas_call x2, Pallas kernels, attend_block(): pl.pallas_call(functools.partial(attend_kernel, cross, images, rows // im...  37.5 us
    pallas_call x2, Pallas kernels, scores_grad(): pl.pallas_call(functools.partial(scores_grad_kernel, cross, images, rows...  26.9 us
    pallas_call x2, Pallas kernels, project_grad(): pl.pallas_call(functools.partial(project_grad_kernel, cross), out_shape=[...  22.5 us
    pallas_call x2, Pallas kernels, matrix_grads(): pl.pallas_call(functools.partial(matrix_grad_kernel, cross, depth), out_s...  22.4 us
    unnamed x152, local copies, waits for them, and re-layouts  20.8 us
  transfers between devices with their start and end apart: 66, of which 27 were waited for; matrix products, arithmetic and copies ran while one was open for 9% of the time, Pallas kernels for 30%

profile of v1, /device:TPU:0, one launch (start us, length us, event | category | flops | bytes accessed | tf_op | source)
XLA Modules:
  0.0 489.3 jit_solution(16318523239685141278)
XLA Ops:
  12.6 4.1 collective-permute-start
  16.8 1.7 collective-permute-start.2
  18.5 1.5 collective-permute-start.3
  20.7 3.0 collective-permute-done.4
  24.2 3.0 collective-permute-done.5
  27.4 4.2 collective-permute-done.6
  31.7 2.6 collective-permute-done.1
  36.5 1.6 collective-permute-start.9
  38.1 1.6 collective-permute-start.10
  39.7 2.1 collective-permute-start.11
  41.8 10.3 %collective-permute-done.11 = bf16[4,128]{1,0:T(4,128)(2,1)S(1)} collective-permute-done((bf16[4,128]{1,0:T(4,128)(2,1)S(1)}, bf16[4,128]{1,0:T(4,128)(2,1)S(1)}, u32[]{:S(2)}, u32[]{:S(2)}) %collective-permute-start.11) | collective-permute-done | bytes 1056 | tf_op jit(solution)/shard_map/ppermute | solution.py:42
  56.3 1.5 collective-permute-start.13
  60.0 3.3 collective-permute-start.14
  63.3 1.6 pad_maximum_fusion.11
  66.4 3.0 collective-permute-start.16
  70.9 9.1 %collective-permute-done.16 = bf16[8,128]{1,0:T(8,128)(2,1)S(1)} collective-permute-done((bf16[8,128]{1,0:T(8,128)(2,1)S(1)}, bf16[8,128]{1,0:T(8,128)(2,1)S(1)}, u32[]{:S(2)}, u32[]{:S(2)}) %collective-permute-start.16) | collective-permute-done | bytes 2080 | tf_op jit(solution)/shard_map/ppermute | solution.py:42
  80.1 13.2 %collective-permute-done.14 = bf16[4,32,1024]{2,1,0:T(8,128)(2,1)} collective-permute-done((bf16[4,32,1024]{2,1,0:T(8,128)(2,1)}, bf16[4,32,1024]{2,1,0:T(8,128)(2,1)}, u32[]{:S(2)}, u32[]{:S(2)}) %collective-permute-start.14) | collective-permute-done | bytes 262176 | tf_op jit(solution)/shard_map/ppermute | solution.py:42
  93.3 3.8 collective-permute-done.15
  104.7 19.8 %collective-permute-done.20.refs_9_ = bf16[8,32,1024]{2,1,0:T(8,128)(2,1)S(1)} collective-permute-done((bf16[8,32,1024]{2,1,0:T(8,128)(2,1)S(1)}, bf16[8,32,1024]{2,1,0:T(8,128)(2,1)S(1)}, u32[]{:S(2)}, u32[]{:S(2)}) %collective-permute-start.20) | collective-permute-done | bytes 524320 | tf_op jit(solution)/shard_map/ppermute | solution.py:42
  124.4 19.3 %collective-permute-done.21.refs_7_ = bf16[8,32,1024]{2,1,0:T(8,128)(2,1)S(1)} collective-permute-done((bf16[8,32,1024]{2,1,0:T(8,128)(2,1)S(1)}, bf16[8,32,1024]{2,1,0:T(8,128)(2,1)S(1)}, u32[]{:S(2)}, u32[]{:S(2)}) %collective-permute-start.21) | collective-permute-done | bytes 524320 | tf_op jit(solution)/shard_map/ppermute | solution.py:42
  143.7 3.7 collective-permute-done.19.refs_3_
  148.5 2.5 collective-permute-done.24.refs_10_
  152.1 2.3 collective-permute-done.25.refs_11_
  157.3 19.3 %shard_map.349 = (bf16[768,1024]{1,0:T(8,128)(2,1)S(1)}, bf16[768,1024]{1,0:T(8,128)(2,1)S(1)}, bf16[768,1024]{1,0:T(8,128)(2,1)}, bf16[768,1024]{1,0:T(8,128)(2...) custom-call(s32[3]{0:T(128)S(1)} %dynamic_slice.3.refs_0_, ...), custom_call_target="tpu_custom_call" | custom-call | flops 7247757312 | bytes 17825792 | tf_op jit(solution)/shard_map/pallas_call | solution.py:364
  178.9 18.2 %shard_map.350 = (bf16[768,1024]{1,0:T(8,128)(2,1)S(1)}, bf16[768,1024]{1,0:T(8,128)(2,1)S(1)}, bf16[768,1024]{1,0:T(8,128)(2,1)}, bf16[768,1024]{1,0:T(8,128)(2...) custom-call(f32[4,1024]{1,0:T(4,128)S(1)} %reshape.238.refs_1_.refs_0_, ...), custom_call_target="tpu_custom_call" | custom-call | flops 7247757312 | bytes 17825792 | tf_op jit(solution)/shard_map/pallas_call | solution.py:364
  199.5 1.9 all-gather.3.cloned.1.call-done
  201.3 20.4 %shard_map.351 = (bf16[768,1024]{1,0:T(8,128)(2,1)}, f32[768,1024]{1,0:T(8,128)}, bf16[768,2048]{1,0:T(8,128)(2,1)}, bf16[2,16,32,1024]{3,2,1,0:T(8,128)(2,1)}, bf16[2,16,32,1024]{3,2,1,0:T(8,128)(2,1)}) custom-call(f32[768,1024]{1,0:T(8,128)} %get-tuple-element.209.second, bf16[768,1024]{1,0:T(8,128)(2,1)} %bitcast.227, f32[1,1024]{1,0:T(1,128)} %slice.346.refs_0_.gain_row, ...), custom_call_target="tpu_custom_call" | custom-call | flops 12884901888 | bytes 25165824 | tf_op jit(solution)/shard_map/pallas_call | solution.py:714
  222.0 18.9 %shard_map.352 = (bf16[768,1024]{1,0:T(8,128)(2,1)}, bf16[768,2048]{1,0:T(8,128)(2,1)}, bf16[2,16,32,1024]{3,2,1,0:T(8,128)(2,1)}, bf16[2,16,32,1024]{3,2,1,0:T(8,128)(2,1)}) custom-call(f32[768,1024]{1,0:T(8,128)} %get-tuple-element.212.second, bf16[768,1024]{1,0:T(8,128)(2,1)} %bitcast.228, bf16[768,1024]{1,0:T(8,128)(2,1)} %get-tuple-element.213.refs_0_.normal, ...), custom_call_target="tpu_custom_call" | custom-call | flops 12884901888 | bytes 25165824 | tf_op jit(solution)/shard_map/pallas_call | solution.py:714
  242.3 1.5 collective-permute-start.31
  244.4 20.3 %shard_map.353 = (f32[768,1024]{1,0:T(8,128)}, f32[1,1024]{1,0:T(1,128)}, bf16[2,16,512,128]{3,2,1,0:T(8,128)(2,1)}, bf16[2,16,512,128]{3,2,1,0:T(8,128)(2,1)}) custom-call(f32[1,1024]{1,0:T(1,128)} %slice.346.refs_0_.gain_row, f32[768,1024]{1,0:T(8,128)} %get-tuple-element.209.second, bf16[768,1024]{1,0:T(8,128)(2,1)} %bitcast.229, ...), custom_call_target="tpu_custom_call" | custom-call | flops 12884901888 | bytes 32505856 | tf_op jit(solution)/shard_map/pallas_call | solution.py:812
  265.6 1.5 collective-permute-start.34
  267.1 3.2 add_convert_fusion.20
  273.1 13.2 %shard_map.354 = (bf16[768,1024]{1,0:T(8,128)(2,1)S(1)}, bf16[768,1024]{1,0:T(8,128)(2,1)S(1)}, bf16[768,1024]{1,0:T(8,128)(2,1)S(1)}) custom-call(f32[768,1024]{1,0:T(8,128)} %get-tuple-element.234.refs_0_.refs_2_, bf16[768,1024]{1,0:T(8,128)(2,1)} %copy-done.7, bf16[768,1024]{1,0:T(8,128)(2,1)} %copy-done.8, bf16[768,1024]{1,0:T(8,128)(2,1)} %get-tuple-element.237.refs_3_, ...), custom_call_target="tpu_custom_call" | custom-call | flops 3623878656 | bytes 18350080 | tf_op jit(solution)/shard_map/pallas_call | solution.py:430
  287.4 2.7 collective-permute-done.35
  292.3 1.6 collective-permute-start.40
  294.6 11.4 %shard_map.355 = (bf16[2,16,64,1024]{3,2,1,0:T(8,128)(2,1)}, bf16[2,16,64,1024]{3,2,1,0:T(8,128)(2,1)}) custom-call(f32[4,1024]{1,0:T(4,128)S(1)} %reshape.238.refs_1_.refs_0_, f32[768,1024]{1,0:T(8,128)} %get-tuple-element.204.refs_1_, f32[768,1024]{1,0:T(8,128)} %get-tuple-element.234.refs_0_.refs_2_, bf16[768,1024]{1,0:T(8,128)(2,1)S(1)} %copy-done.6, ...), custom_call_target="tpu_custom_call" | custom-call | flops 6442450944 | bytes 20971520 | tf_op jit(solution)/shard_map/pallas_call | solution.py:522
  306.7 2.8 add_convert_fusion.8
  309.5 1.5 collective-permute-start.44
  311.6 2.3 collective-permute-start.42
  315.2 12.0 %shard_map.356 = (f32[768,1024]{1,0:T(8,128)}, f32[1,1024]{1,0:T(1,128)S(1)}) custom-call(f32[4,1024]{1,0:T(4,128)S(1)} %reshape.238.refs_1_.refs_0_, f32[768,1024]{1,0:T(8,128)} %get-tuple-element.204.refs_1_, f32[768,1024]{1,0:T(8,128)} %get-tuple-element.234.refs_0_.refs_2_, bf16[768,1024]{1,0:T(8,128)(2,1)S(1)} %get-tuple-element.249.refs_4_.refs_3_, ...), custom_call_target="tpu_custom_call" | custom-call | flops 4831838208 | bytes 22020096 | tf_op jit(solution)/shard_map/pallas_call | solution.py:599
  327.2 8.0 %collective-permute-done.44 = bf16[8,512,128]{2,1,0:T(8,128)(2,1)S(1)} collective-permute-done((bf16[8,512,128]{2,1,0:T(8,128)(2,1)S(1)}, bf16[8,512,128]{2,1,0:T(8,128)(2,1)S(1)}, u32[]{:S(2)}, u32[]{:S(2)}) %collective-permute-start.44) | collective-permute-done | bytes 1048608 | tf_op jit(solution)/shard_map/ppermute | solution.py:42
  336.4 2.5 collective-permute-start.47
  340.3 3.5 add_convert_fusion.4
  343.7 1.6 collective-permute-start.51
  345.3 1.7 collective-permute-start.52
  347.0 13.7 %shard_map.357 = (bf16[768,1024]{1,0:T(8,128)(2,1)S(1)}, bf16[768,1024]{1,0:T(8,128)(2,1)S(1)}, bf16[768,1024]{1,0:T(8,128)(2,1)S(1)}) custom-call(s32[3]{0:T(128)S(1)} %dynamic_slice.3.refs_0_, f32[768,1024]{1,0:T(8,128)} %get-tuple-element.263.refs_1_.refs_3_, bf16[768,1024]{1,0:T(8,128)(2,1)} %copy-done.12, bf16[768,1024]{1,0:T(8,128)(2,1)} %copy-done.13, ...), custom_call_target="tpu_custom_call" | custom-call | flops 3623878656 | bytes 18350080 | tf_op jit(solution)/shard_map/pallas_call | solution.py:430
  363.1 1.8 fusion.26
  367.0 11.0 %shard_map.358 = (bf16[2,16,64,1024]{3,2,1,0:T(8,128)(2,1)}, bf16[2,16,64,1024]{3,2,1,0:T(8,128)(2,1)}) custom-call(f32[4,1024]{1,0:T(4,128)S(1)} %reshape.238.refs_1_.refs_0_, bf16[768,1024]{1,0:T(8,128)(2,1)S(1)} %bitcast.212, bf16[768,1024]{1,0:T(8,128)(2,1)S(1)} %bitcast.215, f32[768,1024]{1,0:T(8,128)} %get-tuple-element.263.refs_1_.refs_3_, ...), custom_call_target="tpu_custom_call" | custom-call | flops 6442450944 | bytes 20971520 | tf_op jit(solution)/shard_map/pallas_call | solution.py:522
  382.5 1.8 collective-permute-start.53
  384.3 10.6 %shard_map.359 = (f32[768,1024]{1,0:T(8,128)}, f32[768,1024]{1,0:T(8,128)}, f32[1,1024]{1,0:T(1,128)S(1)}, f32[1,1024]{1,0:T(1,128)S(1)}) custom-call(f32[4,1024]{1,0:T(4,128)S(1)} %reshape.238.refs_1_.refs_0_, bf16[768,1024]{1,0:T(8,128)(2,1)S(1)} %bitcast.213, bf16[768,1024]{1,0:T(8,128)(2,1)S(1)} %bitcast.216, ...), custom_call_target="tpu_custom_call" | custom-call | flops 4831838208 | bytes 22020096 | tf_op jit(solution)/shard_map/pallas_call | solution.py:599
  394.9 2.3 collective-permute-done.53
  400.2 2.0 add_convert_fusion
  403.7 1.5 collective-permute-start.60
  406.2 7.3 %collective-permute-done.57 = bf16[2,2,64,1024]{3,2,0,1:T(8,128)(2,1)S(1)} collective-permute-done((bf16[2,2,64,1024]{3,2,0,1:T(8,128)(2,1)S(1)}, bf16[2,2,64,1024]{3,2,0,1:T(8,128)(2,1)S(1)}, u32[]{:S(2)}, u32[]{:S(2)}) %collective-permute-start.57) | collective-permute-done | bytes 524320 | tf_op jit(solution)/shard_map/ppermute | solution.py:42
  413.9 13.3 %collective-permute-done.58 = bf16[1,2,64,1024]{3,2,0,1:T(8,128)(2,1)S(1)} collective-permute-done((bf16[1,2,64,1024]{3,2,0,1:T(8,128)(2,1)S(1)}, bf16[1,2,64,1024]{3,2,0,1:T(8,128)(2,1)S(1)}, u32[]{:S(2)}, u32[]{:S(2)}) %collective-permute-start.58) | collective-permute-done | bytes 262176 | tf_op jit(solution)/shard_map/ppermute | solution.py:42
  434.8 2.8 all-to-all-start.1
  437.6 2.1 fusion.57
  439.7 3.6 collective-permute-done.61
  443.3 1.9 collective-permute-done.62
  449.2 3.6 all-to-all-start
  453.0 2.6 multiply_subtract_fusion.2
  457.1 20.4 %all-to-all-done = bf16[4,2,64,1024]{3,2,1,0:T(8,128)(2,1)S(1)} async-done(((bf16[4,2,64,1024]{3,2,1,0:T(8,128)(2,1)}), bf16[4,2,64,1024]{3,2,1,0:T(8,128)(2,1)S(1)}, u32[]{:S(2)}, u32[]{:S(2)}) %all-to-all-start) | async-done | bytes 1048608 | tf_op jit(solution)/shard_map/all_to_all | solution.py:113
  478.4 1.9 multiply_subtract_fusion.3
  480.4 1.8 multiply_subtract_fusion
  (323 shorter events, 78.8 us)
Async XLA Ops:
  7.2 194.1 %all-gather.3.cloned.1.call-start = ((), (), s32[]{:S(2)}) async-start(), calls=%async_computation.2 | async-start | bytes 17301504 | tf_op jit(solution)/shard_map/all_gather | solution.py:888
  12.6 19.1 %collective-permute-start = (bf16[1,96,1024]{2,1,0:T(8,128)(2,1)S(1)}, bf16[1,96,1024]{2,1,0:T(8,128)(2,1)S(1)}, u32[]{:S(2)}, u32[]{:S(2)}) collective-permute-start(bf16[1,96,1024]{2,1,0:T(8,128)(2,1)S(1)} %get-tuple-element.165), channel_id=1, source_target_pairs={{0,2},{1,3},{2,0},{3,1},{4,6},{5,7},{6,4},{7,5},{8,10},{9,11},{10,... | collective-permute-start | bytes 589832 | tf_op jit(solution)/shard_map/ppermute | solution.py:42
  16.7 17.5 %collective-permute-start.1 = (bf16[1,96,1024]{2,1,0:T(8,128)(2,1)S(1)}, bf16[1,96,1024]{2,1,0:T(8,128)(2,1)S(1)}, u32[]{:S(2)}, u32[]{:S(2)}) collective-permute-start(bf16[1,96,1024]{2,1,0:T(8,128)(2,1)S(1)} %get-tuple-element.166), channel_id=1, source_target_pairs={{0,2},{1,3},{2,0},{3,1},{4,6},{5,7},{6,4},{7,5},{8,10},{9,11},{10,... | collective-permute-start | bytes 589832 | tf_op jit(solution)/shard_map/ppermute | solution.py:42
  16.8 14.9 %collective-permute-start.2 = (bf16[1,32,1024]{2,1,0:T(8,128)(2,1)S(1)}, bf16[1,32,1024]{2,1,0:T(8,128)(2,1)S(1)}, u32[]{:S(2)}, u32[]{:S(2)}) collective-permute-start(bf16[1,32,1024]{2,1,0:T(8,128)(2,1)S(1)} %get-tuple-element.167), channel_id=1, source_target_pairs={{0,8},{1,9},{2,10},{3,11},{4,12},{5,13},{6,14},{7,15},{8,0},{9,1},... | collective-permute-start | bytes 196616 | tf_op jit(solution)/shard_map/ppermute | solution.py:42
  18.5 13.1 %collective-permute-start.3 = (bf16[1,32,1024]{2,1,0:T(8,128)(2,1)S(1)}, bf16[1,32,1024]{2,1,0:T(8,128)(2,1)S(1)}, u32[]{:S(2)}, u32[]{:S(2)}) collective-permute-start(bf16[1,32,1024]{2,1,0:T(8,128)(2,1)S(1)} %get-tuple-element.168), channel_id=1, source_target_pairs={{0,16},{1,17},{2,18},{3,19},{4,20},{5,21},{6,22},{7,23},{8,24},{9,... | collective-permute-start | bytes 196616 | tf_op jit(solution)/shard_map/ppermute | solution.py:42
  20.1 3.5 collective-permute-start.4
  23.7 3.5 collective-permute-start.5
  27.2 4.4 collective-permute-start.6
  34.3 17.8 %collective-permute-start.7 = (bf16[2,96,1024]{2,1,0:T(8,128)(2,1)S(1)}, bf16[2,96,1024]{2,1,0:T(8,128)(2,1)S(1)}, u32[]{:S(2)}, u32[]{:S(2)}) collective-permute-start(bf16[2,96,1024]{2,1,0:T(8,128)(2,1)S(1)} %pad_maximum_fusion.6), channel_id=1, source_target_pairs={{0,1},{1,0},{2,3},{3,2},{4,5},{5,4},{6,7},{7,6},{8,9},{9,8},{10,11... | collective-permute-start | bytes 1179656 | tf_op jit(solution)/shard_map/ppermute | solution.py:42
  35.1 18.0 %collective-permute-start.8 = (bf16[2,96,1024]{2,1,0:T(8,128)(2,1)S(1)}, bf16[2,96,1024]{2,1,0:T(8,128)(2,1)S(1)}, u32[]{:S(2)}, u32[]{:S(2)}) collective-permute-start(bf16[2,96,1024]{2,1,0:T(8,128)(2,1)S(1)} %pad_maximum_fusion.7), channel_id=1, source_target_pairs={{0,1},{1,0},{2,3},{3,2},{4,5},{5,4},{6,7},{7,6},{8,9},{9,8},{10,11... | collective-permute-start | bytes 1179656 | tf_op jit(solution)/shard_map/ppermute | solution.py:42
  36.5 15.6 %collective-permute-start.9 = (bf16[2,32,1024]{2,1,0:T(8,128)(2,1)S(1)}, bf16[2,32,1024]{2,1,0:T(8,128)(2,1)S(1)}, u32[]{:S(2)}, u32[]{:S(2)}) collective-permute-start(bf16[2,32,1024]{2,1,0:T(8,128)(2,1)S(1)} %pad_maximum_fusion.12), channel_id=1, source_target_pairs={{0,16},{1,17},{2,18},{3,19},{4,20},{5,21},{6,22},{7,23},{8,24},{9,... | collective-permute-start | bytes 393224 | tf_op jit(solution)/shard_map/ppermute | solution.py:42
  38.1 13.9 %collective-permute-start.10 = (bf16[2,32,1024]{2,1,0:T(8,128)(2,1)S(1)}, bf16[2,32,1024]{2,1,0:T(8,128)(2,1)S(1)}, u32[]{:S(2)}, u32[]{:S(2)}) collective-permute-start(bf16[2,32,1024]{2,1,0:T(8,128)(2,1)S(1)} %pad_maximum_fusion.13), channel_id=1, source_target_pairs={{0,8},{1,9},{2,10},{3,11},{4,12},{5,13},{6,14},{7,15},{8,0},{9,1},... | collective-permute-start | bytes 393224 | tf_op jit(solution)/shard_map/ppermute | solution.py:42
  39.7 12.4 %collective-permute-start.11 = (bf16[4,128]{1,0:T(4,128)(2,1)S(1)}, bf16[4,128]{1,0:T(4,128)(2,1)S(1)}, u32[]{:S(2)}, u32[]{:S(2)}) collective-permute-start(bf16[4,128]{1,0:T(4,128)(2,1)S(1)} %pad_maximum_fusion.15), channel_id=1, source_target_pairs={{0,2},{1,3},{2,0},{3,1},{4,6},{5,7},{6,4},{7,5},{8,10},{9,11},{10,... | collective-permute-start | bytes 3080 | tf_op jit(solution)/shard_map/ppermute | solution.py:42
  54.1 42.9 %collective-permute-start.12 = (bf16[4,96,1024]{2,1,0:T(8,128)(2,1)}, bf16[4,96,1024]{2,1,0:T(8,128)(2,1)S(1)}, u32[]{:S(2)}, u32[]{:S(2)}) collective-permute-start(bf16[4,96,1024]{2,1,0:T(8,128)(2,1)} %pad_maximum_fusion.1), channel_id=1, source_target_pairs={{0,8},{1,9},{2,10},{3,11},{4,12},{5,13},{6,14},{7,15},{8,0},{9,1},... | collective-permute-start | bytes 2359304 | tf_op jit(solution)/shard_map/ppermute | solution.py:42
  56.3 40.7 %collective-permute-start.13 = (bf16[4,96,1024]{2,1,0:T(8,128)(2,1)}, bf16[4,96,1024]{2,1,0:T(8,128)(2,1)S(1)}, u32[]{:S(2)}, u32[]{:S(2)}) collective-permute-start(bf16[4,96,1024]{2,1,0:T(8,128)(2,1)} %pad_maximum_fusion.2), channel_id=1, source_target_pairs={{0,16},{1,17},{2,18},{3,19},{4,20},{5,21},{6,22},{7,23},{8,24},{9,... | collective-permute-start | bytes 2359304 | tf_op jit(solution)/shard_map/ppermute | solution.py:42
  60.0 33.3 %collective-permute-start.14 = (bf16[4,32,1024]{2,1,0:T(8,128)(2,1)}, bf16[4,32,1024]{2,1,0:T(8,128)(2,1)}, u32[]{:S(2)}, u32[]{:S(2)}) collective-permute-start(bf16[4,32,1024]{2,1,0:T(8,128)(2,1)} %pad_maximum_fusion.10), channel_id=1, source_target_pairs={{0,2},{1,3},{2,0},{3,1},{4,6},{5,7},{6,4},{7,5},{8,10},{9,11},{10,... | collective-permute-start | bytes 786440 | tf_op jit(solution)/shard_map/ppermute | solution.py:42
  65.0 32.0 %collective-permute-start.15 = (bf16[4,32,1024]{2,1,0:T(8,128)(2,1)}, bf16[4,32,1024]{2,1,0:T(8,128)(2,1)S(1)}, u32[]{:S(2)}, u32[]{:S(2)}) collective-permute-start(bf16[4,32,1024]{2,1,0:T(8,128)(2,1)} %pad_maximum_fusion.11), channel_id=1, source_target_pairs={{0,2},{1,3},{2,0},{3,1},{4,6},{5,7},{6,4},{7,5},{8,10},{9,11},{10,... | collective-permute-start | bytes 786440 | tf_op jit(solution)/shard_map/ppermute | solution.py:42
  66.4 13.7 %collective-permute-start.16 = (bf16[8,128]{1,0:T(8,128)(2,1)S(1)}, bf16[8,128]{1,0:T(8,128)(2,1)S(1)}, u32[]{:S(2)}, u32[]{:S(2)}) collective-permute-start(bf16[8,128]{1,0:T(8,128)(2,1)S(1)} %concatenate.77), channel_id=1, source_target_pairs={{0,1},{1,0},{2,3},{3,2},{4,5},{5,4},{6,7},{7,6},{8,9},{9,8},{10,11... | collective-permute-start | bytes 6152 | tf_op jit(solution)/shard_map/ppermute | solution.py:42
  98.0 45.8 %collective-permute-start.18 = (bf16[8,96,1024]{2,1,0:T(8,128)(2,1)}, bf16[8,96,1024]{2,1,0:T(8,128)(2,1)}, u32[]{:S(2)}, u32[]{:S(2)}) collective-permute-start(bf16[8,96,1024]{2,1,0:T(8,128)(2,1)} %constant_dynamic-update-slice_fusion.refs_4_), channel_id=1, source_target_pairs={{0,16},{1,17},{2,18},{3,19},{4,20},{5,21},{6,22},{7,23},{8,24},{9,... | collective-permute-start | bytes 4718600 | tf_op jit(solution)/shard_map/ppermute | solution.py:42
  99.5 48.0 %collective-permute-start.19 = (bf16[8,96,1024]{2,1,0:T(8,128)(2,1)}, bf16[8,96,1024]{2,1,0:T(8,128)(2,1)}, u32[]{:S(2)}, u32[]{:S(2)}) collective-permute-start(bf16[8,96,1024]{2,1,0:T(8,128)(2,1)} %constant_dynamic-update-slice_fusion.4.refs_2_), channel_id=1, source_target_pairs={{0,8},{1,9},{2,10},{3,11},{4,12},{5,13},{6,14},{7,15},{8,0},{9,1},... | collective-permute-start | bytes 4718600 | tf_op jit(solution)/shard_map/ppermute | solution.py:42
  101.1 23.4 %collective-permute-start.20 = (bf16[8,32,1024]{2,1,0:T(8,128)(2,1)S(1)}, bf16[8,32,1024]{2,1,0:T(8,128)(2,1)S(1)}, u32[]{:S(2)}, u32[]{:S(2)}) collective-permute-start(bf16[8,32,1024]{2,1,0:T(8,128)(2,1)S(1)} %constant_dynamic-update-slice_fusion.8.refs_8_), channel_id=1, source_target_pairs={{0,1},{1,0},{2,3},{3,2},{4,5},{5,4},{6,7},{7,6},{8,9},{9,8},{10,11... | collective-permute-start | bytes 1572872 | tf_op jit(solution)/shard_map/ppermute | solution.py:42
  102.0 41.8 %collective-permute-start.21 = (bf16[8,32,1024]{2,1,0:T(8,128)(2,1)S(1)}, bf16[8,32,1024]{2,1,0:T(8,128)(2,1)S(1)}, u32[]{:S(2)}, u32[]{:S(2)}) collective-permute-start(bf16[8,32,1024]{2,1,0:T(8,128)(2,1)S(1)} %constant_dynamic-update-slice_fusion.12.refs_6_), channel_id=1, source_target_pairs={{0,1},{1,0},{2,3},{3,2},{4,5},{5,4},{6,7},{7,6},{8,9},{9,8},{10,11... | collective-permute-start | bytes 1572872 | tf_op jit(solution)/shard_map/ppermute | solution.py:42
  104.5 47.4 %collective-permute-start.17 = (bf16[8,96,1024]{2,1,0:T(8,128)(2,1)}, bf16[8,96,1024]{2,1,0:T(8,128)(2,1)}, u32[]{:S(2)}, u32[]{:S(2)}) collective-permute-start(bf16[8,96,1024]{2,1,0:T(8,128)(2,1)} %constant_dynamic-update-slice_fusion.refs_4_), channel_id=1, source_target_pairs={{0,4},{1,5},{2,6},{3,7},{4,0},{5,1},{6,2},{7,3},{8,12},{9,13},{10,... | collective-permute-start | bytes 4718600 | tf_op jit(solution)/shard_map/ppermute | solution.py:42
  147.5 8.1 %collective-permute-start.23 = (bf16[8,96,1024]{2,1,0:T(8,128)(2,1)}, bf16[8,96,1024]{2,1,0:T(8,128)(2,1)}, u32[]{:S(2)}, u32[]{:S(2)}) collective-permute-start(bf16[8,96,1024]{2,1,0:T(8,128)(2,1)} %collective-permute-done.18.refs_5_), channel_id=1, source_target_pairs={{0,4},{1,5},{2,6},{3,7},{4,0},{5,1},{6,2},{7,3},{8,12},{9,13},{10,... | collective-permute-start | bytes 4718600 | tf_op jit(solution)/shard_map/ppermute | solution.py:42
  147.5 3.5 collective-permute-start.24
  148.0 30.9 %collective-permute-start.26 = (bf16[8,96,1024]{2,1,0:T(8,128)(2,1)}, bf16[8,96,1024]{2,1,0:T(8,128)(2,1)}, u32[]{:S(2)}, u32[]{:S(2)}) collective-permute-start(bf16[8,96,1024]{2,1,0:T(8,128)(2,1)} %constant_dynamic-update-slice_fusion.4.refs_2_), channel_id=1, source_target_pairs={{0,4},{1,5},{2,6},{3,7},{4,0},{5,1},{6,2},{7,3},{8,12},{9,13},{10,... | collective-permute-start | bytes 4718600 | tf_op jit(solution)/shard_map/ppermute | solution.py:42
  148.0 30.9 %collective-permute-start.27 = (bf16[8,96,1024]{2,1,0:T(8,128)(2,1)}, bf16[8,96,1024]{2,1,0:T(8,128)(2,1)}, u32[]{:S(2)}, u32[]{:S(2)}) collective-permute-start(bf16[8,96,1024]{2,1,0:T(8,128)(2,1)} %collective-permute-done.19.refs_3_), channel_id=1, source_target_pairs={{0,4},{1,5},{2,6},{3,7},{4,0},{5,1},{6,2},{7,3},{8,12},{9,13},{10,... | collective-permute-start | bytes 4718600 | tf_op jit(solution)/shard_map/ppermute | solution.py:42
  151.9 27.0 %collective-permute-start.28 = (bf16[8,32,1024]{2,1,0:T(8,128)(2,1)S(1)}, bf16[8,32,1024]{2,1,0:T(8,128)(2,1)S(1)}, u32[]{:S(2)}, u32[]{:S(2)}) collective-permute-start(bf16[8,32,1024]{2,1,0:T(8,128)(2,1)S(1)} %constant_dynamic-update-slice_fusion.12.refs_6_), channel_id=1, source_target_pairs={{0,4},{1,5},{2,6},{3,7},{4,0},{5,1},{6,2},{7,3},{8,12},{9,13},{10,... | collective-permute-start | bytes 1572872 | tf_op jit(solution)/shard_map/ppermute | solution.py:42
  155.2 23.7 %collective-permute-start.29 = (bf16[8,32,1024]{2,1,0:T(8,128)(2,1)S(1)}, bf16[8,32,1024]{2,1,0:T(8,128)(2,1)S(1)}, u32[]{:S(2)}, u32[]{:S(2)}) collective-permute-start(bf16[8,32,1024]{2,1,0:T(8,128)(2,1)S(1)} %collective-permute-done.21.refs_7_), channel_id=1, source_target_pairs={{0,4},{1,5},{2,6},{3,7},{4,0},{5,1},{6,2},{7,3},{8,12},{9,13},{10,... | collective-permute-start | bytes 1572872 | tf_op jit(solution)/shard_map/ppermute | solution.py:42
  221.7 19.2 %collective-permute-start.30 = (bf16[2,16,32,1024]{3,2,1,0:T(8,128)(2,1)}, bf16[2,16,32,1024]{3,2,1,0:T(8,128)(2,1)S(1)}, u32[]{:S(2)}, u32[]{:S(2)}) collective-permute-start(bf16[2,16,32,1024]{3,2,1,0:T(8,128)(2,1)} %get-tuple-element.211), channel_id=1, source_target_pairs={{0,4},{1,5},{2,6},{3,7},{4,0},{5,1},{6,2},{7,3},{8,12},{9,13},{10,... | collective-permute-start | bytes 6291464 | tf_op jit(solution)/shard_map/ppermute | solution.py:42
  240.9 23.8 %collective-permute-start.33 = (bf16[2,16,32,1024]{3,2,1,0:T(8,128)(2,1)}, bf16[2,16,32,1024]{3,2,1,0:T(8,128)(2,1)}, u32[]{:S(2)}, u32[]{:S(2)}) collective-permute-start(bf16[2,16,32,1024]{3,2,1,0:T(8,128)(2,1)} %get-tuple-element.221), channel_id=1, source_target_pairs={{0,4},{1,5},{2,6},{3,7},{4,0},{5,1},{6,2},{7,3},{8,12},{9,13},{10,... | collective-permute-start | bytes 6291464 | tf_op jit(solution)/shard_map/ppermute | solution.py:42
  242.3 22.4 %collective-permute-start.31 = (bf16[8,32,1024]{2,1,0:T(8,128)(2,1)S(1)}, bf16[8,32,1024]{2,1,0:T(8,128)(2,1)S(1)}, u32[]{:S(2)}, u32[]{:S(2)}) collective-permute-start(bf16[8,32,1024]{2,1,0:T(8,128)(2,1)S(1)} %get-tuple-element.345), channel_id=1, source_target_pairs={{0,16},{1,17},{2,18},{3,19},{4,20},{5,21},{6,22},{7,23},{8,24},{9,... | collective-permute-start | bytes 1572872 | tf_op jit(solution)/shard_map/ppermute | solution.py:42
  243.8 20.9 %collective-permute-start.32 = (bf16[8,32,1024]{2,1,0:T(8,128)(2,1)S(1)}, bf16[8,32,1024]{2,1,0:T(8,128)(2,1)S(1)}, u32[]{:S(2)}, u32[]{:S(2)}) collective-permute-start(bf16[8,32,1024]{2,1,0:T(8,128)(2,1)S(1)} %get-tuple-element.344), channel_id=1, source_target_pairs={{0,8},{1,9},{2,10},{3,11},{4,12},{5,13},{6,14},{7,15},{8,0},{9,1},... | collective-permute-start | bytes 1572872 | tf_op jit(solution)/shard_map/ppermute | solution.py:42
  265.5 24.6 %collective-permute-start.38 = (bf16[2,16,512,128]{3,2,1,0:T(8,128)(2,1)}, bf16[2,16,512,128]{3,2,1,0:T(8,128)(2,1)S(1)}, u32[]{:S(2)}, u32[]{:S(2)}) collective-permute-start(bf16[2,16,512,128]{3,2,1,0:T(8,128)(2,1)} %get-tuple-element.233), channel_id=1, source_target_pairs={{0,4},{1,5},{2,6},{3,7},{4,0},{5,1},{6,2},{7,3},{8,12},{9,13},{10,... | collective-permute-start | bytes 12582920 | tf_op jit(solution)/shard_map/ppermute | solution.py:42
  265.6 21.9 %collective-permute-start.34 = (bf16[4,32,1024]{2,1,0:T(8,128)(2,1)S(1)}, bf16[4,32,1024]{2,1,0:T(8,128)(2,1)S(1)}, u32[]{:S(2)}, u32[]{:S(2)}) collective-permute-start(bf16[4,32,1024]{2,1,0:T(8,128)(2,1)S(1)} %fusion.40), channel_id=1, source_target_pairs={{0,8},{1,9},{2,10},{3,11},{4,12},{5,13},{6,14},{7,15},{8,0},{9,1},... | collective-permute-start | bytes 786440 | tf_op jit(solution)/shard_map/ppermute | solution.py:42
  270.3 19.8 %collective-permute-start.36 = (bf16[8,32,1024]{2,1,0:T(8,128)(2,1)S(1)}, bf16[8,32,1024]{2,1,0:T(8,128)(2,1)S(1)}, u32[]{:S(2)}, u32[]{:S(2)}) collective-permute-start(bf16[8,32,1024]{2,1,0:T(8,128)(2,1)S(1)} %get-tuple-element.341), channel_id=1, source_target_pairs={{0,16},{1,17},{2,18},{3,19},{4,20},{5,21},{6,22},{7,23},{8,24},{9,... | collective-permute-start | bytes 1572872 | tf_op jit(solution)/shard_map/ppermute | solution.py:42
  270.9 19.2 %collective-permute-start.37 = (bf16[8,32,1024]{2,1,0:T(8,128)(2,1)S(1)}, bf16[8,32,1024]{2,1,0:T(8,128)(2,1)S(1)}, u32[]{:S(2)}, u32[]{:S(2)}) collective-permute-start(bf16[8,32,1024]{2,1,0:T(8,128)(2,1)S(1)} %get-tuple-element.340), channel_id=1, source_target_pairs={{0,8},{1,9},{2,10},{3,11},{4,12},{5,13},{6,14},{7,15},{8,0},{9,1},... | collective-permute-start | bytes 1572872 | tf_op jit(solution)/shard_map/ppermute | solution.py:42
  272.2 17.9 %collective-permute-start.35 = (bf16[4,32,1024]{2,1,0:T(8,128)(2,1)S(1)}, bf16[4,32,1024]{2,1,0:T(8,128)(2,1)}, u32[]{:S(2)}, u32[]{:S(2)}) collective-permute-start(bf16[4,32,1024]{2,1,0:T(8,128)(2,1)S(1)} %fusion.39), channel_id=1, source_target_pairs={{0,16},{1,17},{2,18},{3,19},{4,20},{5,21},{6,22},{7,23},{8,24},{9,... | collective-permute-start | bytes 786440 | tf_op jit(solution)/shard_map/ppermute | solution.py:42
  291.7 14.2 %collective-permute-start.39 = (bf16[2,2,32,1024]{3,2,1,0:T(8,128)(2,1)S(1)}, bf16[2,2,32,1024]{3,2,1,0:T(8,128)(2,1)S(1)}, u32[]{:S(2)}, u32[]{:S(2)}) collective-permute-start(bf16[2,2,32,1024]{3,2,1,0:T(8,128)(2,1)S(1)} %pad_maximum_fusion.9), channel_id=1, source_target_pairs={{0,1},{1,0},{2,3},{3,2},{4,5},{5,4},{6,7},{7,6},{8,9},{9,8},{10,11... | collective-permute-start | bytes 786440 | tf_op jit(solution)/shard_map/ppermute | solution.py:42
  292.3 13.7 %collective-permute-start.40 = (bf16[4,32,1024]{2,1,0:T(8,128)(2,1)S(1)}, bf16[4,32,1024]{2,1,0:T(8,128)(2,1)S(1)}, u32[]{:S(2)}, u32[]{:S(2)}) collective-permute-start(bf16[4,32,1024]{2,1,0:T(8,128)(2,1)S(1)} %fusion.36), channel_id=1, source_target_pairs={{0,8},{1,9},{2,10},{3,11},{4,12},{5,13},{6,14},{7,15},{8,0},{9,1},... | collective-permute-start | bytes 786440 | tf_op jit(solution)/shard_map/ppermute | solution.py:42
  293.9 12.1 %collective-permute-start.41 = (bf16[4,32,1024]{2,1,0:T(8,128)(2,1)S(1)}, bf16[4,32,1024]{2,1,0:T(8,128)(2,1)S(1)}, u32[]{:S(2)}, u32[]{:S(2)}) collective-permute-start(bf16[4,32,1024]{2,1,0:T(8,128)(2,1)S(1)} %fusion.35), channel_id=1, source_target_pairs={{0,16},{1,17},{2,18},{3,19},{4,20},{5,21},{6,22},{7,23},{8,24},{9,... | collective-permute-start | bytes 786440 | tf_op jit(solution)/shard_map/ppermute | solution.py:42
  306.7 29.6 %collective-permute-start.46 = (bf16[2,16,64,1024]{3,2,1,0:T(8,128)(2,1)}, bf16[2,16,64,1024]{3,2,1,0:T(8,128)(2,1)}, u32[]{:S(2)}, u32[]{:S(2)}) collective-permute-start(bf16[2,16,64,1024]{3,2,1,0:T(8,128)(2,1)} %get-tuple-element.257), channel_id=1, source_target_pairs={{0,4},{1,5},{2,6},{3,7},{4,0},{5,1},{6,2},{7,3},{8,12},{9,13},{10,... | collective-permute-start | bytes 12582920 | tf_op jit(solution)/shard_map/ppermute | solution.py:42
  309.5 25.6 %collective-permute-start.44 = (bf16[8,512,128]{2,1,0:T(8,128)(2,1)S(1)}, bf16[8,512,128]{2,1,0:T(8,128)(2,1)S(1)}, u32[]{:S(2)}, u32[]{:S(2)}) collective-permute-start(bf16[8,512,128]{2,1,0:T(8,128)(2,1)S(1)} %get-tuple-element.336), channel_id=1, source_target_pairs={{0,16},{1,17},{2,18},{3,19},{4,20},{5,21},{6,22},{7,23},{8,24},{9,... | collective-permute-start | bytes 3145736 | tf_op jit(solution)/shard_map/ppermute | solution.py:42
  311.0 25.3 %collective-permute-start.45 = (bf16[8,512,128]{2,1,0:T(8,128)(2,1)S(1)}, bf16[8,512,128]{2,1,0:T(8,128)(2,1)S(1)}, u32[]{:S(2)}, u32[]{:S(2)}) collective-permute-start(bf16[8,512,128]{2,1,0:T(8,128)(2,1)S(1)} %get-tuple-element.335), channel_id=1, source_target_pairs={{0,8},{1,9},{2,10},{3,11},{4,12},{5,13},{6,14},{7,15},{8,0},{9,1},... | collective-permute-start | bytes 3145736 | tf_op jit(solution)/shard_map/ppermute | solution.py:42
  311.6 15.5 %collective-permute-start.42 = (bf16[1,2,32,1024]{3,2,1,0:T(8,128)(2,1)S(1)}, bf16[1,2,32,1024]{3,2,1,0:T(8,128)(2,1)S(1)}, u32[]{:S(2)}, u32[]{:S(2)}) collective-permute-start(bf16[1,2,32,1024]{3,2,1,0:T(8,128)(2,1)S(1)} %slice.460), channel_id=1, source_target_pairs={{0,2},{1,3},{2,0},{3,1},{4,6},{5,7},{6,4},{7,5},{8,10},{9,11},{10,... | collective-permute-start | bytes 393224 | tf_op jit(solution)/shard_map/ppermute | solution.py:42
  314.3 12.9 %collective-permute-start.43 = (bf16[2,2,32,1024]{3,2,0,1:T(8,128)(2,1)S(1)}, bf16[2,2,32,1024]{3,2,0,1:T(8,128)(2,1)S(1)}, u32[]{:S(2)}, u32[]{:S(2)}) collective-permute-start(bf16[2,2,32,1024]{3,2,0,1:T(8,128)(2,1)S(1)} %fusion.49), channel_id=1, source_target_pairs={{0,1},{1,0},{2,3},{3,2},{4,5},{5,4},{6,7},{7,6},{8,9},{9,8},{10,11... | collective-permute-start | bytes 786440 | tf_op jit(solution)/shard_map/ppermute | solution.py:42
  336.4 26.6 %collective-permute-start.47 = (bf16[1,2,32,1024]{3,2,0,1:T(8,128)(2,1)S(1)}, bf16[1,2,32,1024]{3,2,0,1:T(8,128)(2,1)}, u32[]{:S(2)}, u32[]{:S(2)}) collective-permute-start(bf16[1,2,32,1024]{3,2,0,1:T(8,128)(2,1)S(1)} %slice.465), channel_id=1, source_target_pairs={{0,2},{1,3},{2,0},{3,1},{4,6},{5,7},{6,4},{7,5},{8,10},{9,11},{10,... | collective-permute-start | bytes 393224 | tf_op jit(solution)/shard_map/ppermute | solution.py:42
  339.1 24.0 %collective-permute-start.48 = (bf16[4,512,128]{2,1,0:T(8,128)(2,1)S(1)}, bf16[4,512,128]{2,1,0:T(8,128)(2,1)}, u32[]{:S(2)}, u32[]{:S(2)}) collective-permute-start(bf16[4,512,128]{2,1,0:T(8,128)(2,1)S(1)} %fusion.16), channel_id=1, source_target_pairs={{0,8},{1,9},{2,10},{3,11},{4,12},{5,13},{6,14},{7,15},{8,0},{9,1},... | collective-permute-start | bytes 1572872 | tf_op jit(solution)/shard_map/ppermute | solution.py:42
  339.7 23.4 %collective-permute-start.49 = (bf16[4,512,128]{2,1,0:T(8,128)(2,1)S(1)}, bf16[4,512,128]{2,1,0:T(8,128)(2,1)}, u32[]{:S(2)}, u32[]{:S(2)}) collective-permute-start(bf16[4,512,128]{2,1,0:T(8,128)(2,1)S(1)} %fusion.15), channel_id=1, source_target_pairs={{0,16},{1,17},{2,18},{3,19},{4,20},{5,21},{6,22},{7,23},{8,24},{9,... | collective-permute-start | bytes 1572872 | tf_op jit(solution)/shard_map/ppermute | solution.py:42
  343.7 34.6 %collective-permute-start.51 = (bf16[8,64,1024]{2,1,0:T(8,128)(2,1)S(1)}, bf16[8,64,1024]{2,1,0:T(8,128)(2,1)}, u32[]{:S(2)}, u32[]{:S(2)}) collective-permute-start(bf16[8,64,1024]{2,1,0:T(8,128)(2,1)S(1)} %get-tuple-element.333), channel_id=1, source_target_pairs={{0,16},{1,17},{2,18},{3,19},{4,20},{5,21},{6,22},{7,23},{8,24},{9,... | collective-permute-start | bytes 3145736 | tf_op jit(solution)/shard_map/ppermute | solution.py:42
  345.3 33.1 %collective-permute-start.52 = (bf16[8,64,1024]{2,1,0:T(8,128)(2,1)S(1)}, bf16[8,64,1024]{2,1,0:T(8,128)(2,1)}, u32[]{:S(2)}, u32[]{:S(2)}) collective-permute-start(bf16[8,64,1024]{2,1,0:T(8,128)(2,1)S(1)} %get-tuple-element.332), channel_id=1, source_target_pairs={{0,8},{1,9},{2,10},{3,11},{4,12},{5,13},{6,14},{7,15},{8,0},{9,1},... | collective-permute-start | bytes 3145736 | tf_op jit(solution)/shard_map/ppermute | solution.py:42
  366.5 11.9 %collective-permute-start.50 = (bf16[2,2,512,128]{3,2,0,1:T(8,128)(2,1)S(1)}, bf16[2,2,512,128]{3,2,0,1:T(8,128)(2,1)S(1)}, u32[]{:S(2)}, u32[]{:S(2)}) collective-permute-start(bf16[2,2,512,128]{3,2,0,1:T(8,128)(2,1)S(1)} %pad_maximum_fusion.4), channel_id=1, source_target_pairs={{0,1},{1,0},{2,3},{3,2},{4,5},{5,4},{6,7},{7,6},{8,9},{9,8},{10,11... | collective-permute-start | bytes 1572872 | tf_op jit(solution)/shard_map/ppermute | solution.py:42
  378.4 18.8 %collective-permute-start.56 = (bf16[2,16,64,1024]{3,2,1,0:T(8,128)(2,1)}, bf16[2,16,64,1024]{3,2,1,0:T(8,128)(2,1)S(1)}, u32[]{:S(2)}, u32[]{:S(2)}) collective-permute-start(bf16[2,16,64,1024]{3,2,1,0:T(8,128)(2,1)} %get-tuple-element.285), channel_id=1, source_target_pairs={{0,4},{1,5},{2,6},{3,7},{4,0},{5,1},{6,2},{7,3},{8,12},{9,13},{10,... | collective-permute-start | bytes 12582920 | tf_op jit(solution)/shard_map/ppermute | solution.py:42
  379.7 17.5 %collective-permute-start.54 = (bf16[4,64,1024]{2,1,0:T(8,128)(2,1)S(1)}, bf16[4,64,1024]{2,1,0:T(8,128)(2,1)S(1)}, u32[]{:S(2)}, u32[]{:S(2)}) collective-permute-start(bf16[4,64,1024]{2,1,0:T(8,128)(2,1)S(1)} %fusion.13), channel_id=1, source_target_pairs={{0,8},{1,9},{2,10},{3,11},{4,12},{5,13},{6,14},{7,15},{8,0},{9,1},... | collective-permute-start | bytes 1572872 | tf_op jit(solution)/shard_map/ppermute | solution.py:42
  381.6 15.6 %collective-permute-start.55 = (bf16[4,64,1024]{2,1,0:T(8,128)(2,1)S(1)}, bf16[4,64,1024]{2,1,0:T(8,128)(2,1)S(1)}, u32[]{:S(2)}, u32[]{:S(2)}) collective-permute-start(bf16[4,64,1024]{2,1,0:T(8,128)(2,1)S(1)} %fusion.12), channel_id=1, source_target_pairs={{0,16},{1,17},{2,18},{3,19},{4,20},{5,21},{6,22},{7,23},{8,24},{9,... | collective-permute-start | bytes 1572872 | tf_op jit(solution)/shard_map/ppermute | solution.py:42
  382.5 14.7 %collective-permute-start.53 = (bf16[1,2,512,128]{3,2,0,1:T(8,128)(2,1)S(1)}, bf16[1,2,512,128]{3,2,0,1:T(8,128)(2,1)S(1)}, u32[]{:S(2)}, u32[]{:S(2)}) collective-permute-start(bf16[1,2,512,128]{3,2,0,1:T(8,128)(2,1)S(1)} %slice.471), channel_id=1, source_target_pairs={{0,2},{1,3},{2,0},{3,1},{4,6},{5,7},{6,4},{7,5},{8,10},{9,11},{10,... | collective-permute-start | bytes 786440 | tf_op jit(solution)/shard_map/ppermute | solution.py:42
  400.1 13.4 %collective-permute-start.57 = (bf16[2,2,64,1024]{3,2,0,1:T(8,128)(2,1)S(1)}, bf16[2,2,64,1024]{3,2,0,1:T(8,128)(2,1)S(1)}, u32[]{:S(2)}, u32[]{:S(2)}) collective-permute-start(bf16[2,2,64,1024]{3,2,0,1:T(8,128)(2,1)S(1)} %pad_maximum_fusion.3), channel_id=1, source_target_pairs={{0,1},{1,0},{2,3},{3,2},{4,5},{5,4},{6,7},{7,6},{8,9},{9,8},{10,11... | collective-permute-start | bytes 1572872 | tf_op jit(solution)/shard_map/ppermute | solution.py:42
  402.2 25.0 %collective-permute-start.59 = (bf16[8,64,1024]{2,1,0:T(8,128)(2,1)S(1)}, bf16[8,64,1024]{2,1,0:T(8,128)(2,1)S(1)}, u32[]{:S(2)}, u32[]{:S(2)}) collective-permute-start(bf16[8,64,1024]{2,1,0:T(8,128)(2,1)S(1)} %get-tuple-element.328), channel_id=1, source_target_pairs={{0,16},{1,17},{2,18},{3,19},{4,20},{5,21},{6,22},{7,23},{8,24},{9,... | collective-permute-start | bytes 3145736 | tf_op jit(solution)/shard_map/ppermute | solution.py:42
  403.7 24.2 %collective-permute-start.60 = (bf16[8,64,1024]{2,1,0:T(8,128)(2,1)S(1)}, bf16[8,64,1024]{2,1,0:T(8,128)(2,1)S(1)}, u32[]{:S(2)}, u32[]{:S(2)}) collective-permute-start(bf16[8,64,1024]{2,1,0:T(8,128)(2,1)S(1)} %get-tuple-element.327), channel_id=1, source_target_pairs={{0,8},{1,9},{2,10},{3,11},{4,12},{5,13},{6,14},{7,15},{8,0},{9,1},... | collective-permute-start | bytes 3145736 | tf_op jit(solution)/shard_map/ppermute | solution.py:42
  413.8 13.4 %collective-permute-start.58 = (bf16[1,2,64,1024]{3,2,0,1:T(8,128)(2,1)S(1)}, bf16[1,2,64,1024]{3,2,0,1:T(8,128)(2,1)S(1)}, u32[]{:S(2)}, u32[]{:S(2)}) collective-permute-start(bf16[1,2,64,1024]{3,2,0,1:T(8,128)(2,1)S(1)} %slice.479), channel_id=1, source_target_pairs={{0,2},{1,3},{2,0},{3,1},{4,6},{5,7},{6,4},{7,5},{8,10},{9,11},{10,... | collective-permute-start | bytes 786440 | tf_op jit(solution)/shard_map/ppermute | solution.py:42
  429.1 14.2 %collective-permute-start.61 = (bf16[4,64,1024]{2,1,0:T(8,128)(2,1)}, bf16[4,64,1024]{2,1,0:T(8,128)(2,1)}, u32[]{:S(2)}, u32[]{:S(2)}) collective-permute-start(bf16[4,64,1024]{2,1,0:T(8,128)(2,1)} %fusion.8), channel_id=1, source_target_pairs={{0,8},{1,9},{2,10},{3,11},{4,12},{5,13},{6,14},{7,15},{8,0},{9,1},... | collective-permute-start | bytes 1572872 | tf_op jit(solution)/shard_map/ppermute | solution.py:42
  431.4 13.8 %collective-permute-start.62 = (bf16[4,64,1024]{2,1,0:T(8,128)(2,1)}, bf16[4,64,1024]{2,1,0:T(8,128)(2,1)}, u32[]{:S(2)}, u32[]{:S(2)}) collective-permute-start(bf16[4,64,1024]{2,1,0:T(8,128)(2,1)} %fusion.7), channel_id=1, source_target_pairs={{0,16},{1,17},{2,18},{3,19},{4,20},{5,21},{6,22},{7,23},{8,24},{9,... | collective-permute-start | bytes 1572872 | tf_op jit(solution)/shard_map/ppermute | solution.py:42
  434.8 14.5 %all-to-all-start.1 = ((f32[32,1,128]{2,1,0:T(1,128)}), f32[32,1,128]{2,1,0:T(1,128)S(1)}, u32[]{:S(2)}, u32[]{:S(2)}) async-start(f32[32,1,128]{2,1,0:T(1,128)} %bitcast.67), calls=%async_computation.1 | async-start | bytes 32768 | tf_op jit(solution)/shard_map/all_to_all | solution.py:228
  449.2 28.3 %all-to-all-start = ((bf16[4,2,64,1024]{3,2,1,0:T(8,128)(2,1)}), bf16[4,2,64,1024]{3,2,1,0:T(8,128)(2,1)S(1)}, u32[]{:S(2)}, u32[]{:S(2)}) async-start(bf16[4,2,64,1024]{3,2,1,0:T(8,128)(2,1)} %copy.51), calls=%async_computation | async-start | bytes 2097152 | tf_op jit(solution)/shard_map/all_to_all | solution.py:113
  (73 other events, 594.8 us)
Sparse Core Ops, SparseCore 0:
  53.2 148.0 all-gather.2
